TPU v7x, 512 devices: a whole 4x8x8 slice. The times are simulated.
512 devices in a mesh: ens: 4 (over x), grid: 128 (over y, z, core).
Axes of the slice: x: 4, y: 8, z: 8, core: 2. Of those that a mesh axis runs over, the one named last changes fastest.
Arguments:
- grid_latent: bfloat16 [4, 131072, 512], P('ens', 'grid'), may hold values from -6 to 6
- mesh_latent: bfloat16 [4, 16384, 512], P('ens', 'grid'), may hold values from -6 to 6
- cotangent: bfloat16 [4, 16384, 512], P('ens', 'grid'), may hold values from -6 to 6
- edge_weights: bfloat16 [1024, 2, 128, 128], P('grid'), may hold values from -0.125 to 0.125
- edge_targets: int32 [1024, 2], P('grid'), may hold values from 0 to 127, as said below
- mesh_weights: bfloat16 [128, 2, 128, 128], P('grid'), may hold values from -0.375 to 0.375
- mesh_sources: int32 [128, 2], P('grid'), may hold values from 0 to 127, as said below
- encode_weight: bfloat16 [512, 512], replicated, may hold values from -0.25 to 0.25
- aggregate_weight: bfloat16 [512, 512], replicated, may hold values from -0.25 to 0.25
- process_weight: bfloat16 [512, 512], replicated, may hold values from -0.25 to 0.25
Outputs:
- result: bfloat16 [4, 16384, 512], P('ens', 'grid')
- grid_grad: bfloat16 [4, 131072, 512], P('ens', 'grid')
- grad_encode: float32 [512, 512], P('grid')
Inputs may be any that keep to these rules, and one draw needn't show every extreme that they name: `edge_targets`: row b names 2 different mesh blocks, each at most one away from b // 8. `mesh_sources`: row t names 2 different mesh blocks, each at most one away from t.
All inputs are finite; a program needn't handle non-finite values.
Results may differ from a plain program's by a relative error of at most 0.018.
Values may be sent and summed in bfloat16 or wider, within the bound.
No kernel may reach another device: no remote copies, remote signals or barrier semaphores. Data moves between devices by JAX's collectives and lax.ppermute only.
A program may use at most 64 MiB of HBM per device.

v0:
```python
import jax
import jax.numpy as jnp
from jax import lax
from jax.sharding import PartitionSpec as P


def passed_along(value, axis, steps):
    count = lax.axis_size(axis)
    initial, last = (max(0, -steps), min(count, count - steps))
    return lax.ppermute(value, axis, [(source, source + steps) for source in range(initial, last)])


def with_halo(cells, sides, width):
    for axis, dim in sides:
        count = lax.axis_size(axis)
        ends = count - 1
        head = lax.slice_in_dim(cells, 0, width, axis=dim)
        tail = lax.slice_in_dim(cells, cells.shape[dim] - width, cells.shape[dim], axis=dim)
        cells = jnp.concatenate(
            [
                lax.ppermute(tail, axis, [(i, (i + 1) % count) for i in range(ends)]),
                cells,
                lax.ppermute(head, axis, [((i + 1) % count, i) for i in range(ends)]),
            ],
            axis=dim,
        )
    return cells


def silu_slope(value):
    sig = jax.nn.sigmoid(value)
    return sig * (1.0 + value * (1.0 - sig))


def on_device(
    grid_latent,
    mesh_latent,
    cotangent,
    edge_weights,
    edge_targets,
    mesh_weights,
    mesh_sources,
    encode_weight,
    aggregate_weight,
    process_weight,
):
    here = lax.axis_index("grid")
    blocks, slots, rows, unused = edge_weights.shape
    width = grid_latent.shape[2]
    three = jnp.arange(3, dtype=jnp.int32)
    target_pick = ((edge_targets - here + 1)[:, :, None] == three).astype(jnp.bfloat16)
    source_pick = ((mesh_sources[0] - here + 1)[:, None] == three).astype(jnp.bfloat16)
    grid_x = grid_latent[0]
    encoded = jnp.dot(grid_x, encode_weight, preferred_element_type=jnp.float32)
    messages = jax.nn.silu(encoded).astype(jnp.bfloat16).reshape(blocks, rows, width)
    products = jnp.einsum(
        "bkac,bcd->bkad", edge_weights, messages, preferred_element_type=jnp.float32
    )
    panels = jnp.einsum("bkj,bkad->jad", target_pick.astype(jnp.float32), products).astype(
        jnp.bfloat16
    )
    arrived = panels[1].astype(jnp.float32)
    for offset in (1, -1):
        arrived = arrived + passed_along(panels[offset + 1], "grid", offset).astype(jnp.float32)
    aggregated = arrived.astype(jnp.bfloat16)
    mesh_pre = jnp.dot(aggregated, aggregate_weight, preferred_element_type=jnp.float32)
    updated = (mesh_latent[0].astype(jnp.float32) + jax.nn.silu(mesh_pre)).astype(jnp.bfloat16)
    widened = with_halo(updated[None], (("grid", 1),), rows)
    nearby = widened[0].reshape(3, rows, width)
    chosen = jnp.einsum(
        "kj,jbd->kbd", source_pick, nearby, preferred_element_type=jnp.float32
    ).astype(jnp.bfloat16)
    processed = jnp.einsum(
        "kab,kbd->ad", mesh_weights[0], chosen, preferred_element_type=jnp.float32
    ).astype(jnp.bfloat16)
    proc_pre = jnp.dot(processed, process_weight, preferred_element_type=jnp.float32)
    result = (updated.astype(jnp.float32) + jax.nn.silu(proc_pre)).astype(jnp.bfloat16)
    upstream = cotangent[0].astype(jnp.float32)
    proc_delta = (upstream * silu_slope(proc_pre)).astype(jnp.bfloat16)
    proc_back = jnp.einsum(
        "ae,de->ad", proc_delta, process_weight, preferred_element_type=jnp.float32
    ).astype(jnp.bfloat16)
    back = jnp.einsum("kab,ad->kbd", mesh_weights[0], proc_back, preferred_element_type=jnp.float32)
    pushed = jnp.einsum("kj,kbd->jbd", source_pick.astype(jnp.float32), back).astype(jnp.bfloat16)
    mesh_grad = upstream + pushed[1].astype(jnp.float32)
    for offset in (1, -1):
        mesh_grad = mesh_grad + passed_along(pushed[offset + 1], "grid", offset).astype(jnp.float32)
    mesh_delta = (mesh_grad * silu_slope(mesh_pre)).astype(jnp.bfloat16)
    agg_grad = jnp.einsum(
        "ae,de->ad", mesh_delta, aggregate_weight, preferred_element_type=jnp.float32
    ).astype(jnp.bfloat16)
    returned = with_halo(agg_grad[None], (("grid", 1),), rows)
    returned = returned[0].reshape(3, rows, width)
    picked = jnp.einsum(
        "bkj,jad->bkad", target_pick, returned, preferred_element_type=jnp.float32
    ).astype(jnp.bfloat16)
    message_grad = jnp.einsum(
        "bkac,bkad->bcd", edge_weights, picked, preferred_element_type=jnp.float32
    )
    message_grad = message_grad.reshape(blocks * rows, width)
    enc_delta = (message_grad * silu_slope(encoded)).astype(jnp.bfloat16)
    grad_enc = jnp.einsum("rd,re->de", grid_x, enc_delta, preferred_element_type=jnp.float32)
    grid_grad = jnp.einsum(
        "re,de->rd", enc_delta, encode_weight, preferred_element_type=jnp.float32
    ).astype(jnp.bfloat16)
    members = lax.axis_size("ens")
    bands = lax.axis_size("grid")
    grid_scale = 1.0 / float(members * blocks * rows * bands) ** 0.5
    partial_grad = grad_enc * grid_scale
    summed = lax.psum(partial_grad, ("ens", "grid"))
    share = width // bands
    final = lax.dynamic_slice_in_dim(summed, here * share, share, 0)
    return (result[None], grid_grad[None], final)


def solution(mesh):
    return jax.shard_map(
        on_device,
        mesh=mesh,
        in_specs=(
            P("ens", "grid", None),
            P("ens", "grid", None),
            P("ens", "grid", None),
            P("grid", None, None, None),
            P("grid", None),
            P("grid", None, None, None),
            P("grid", None),
            P(),
            P(),
            P(),
        ),
        out_specs=(P("ens", "grid", None), P("ens", "grid", None), P("grid", None)),
        check_vma=False,
    )
```

profile of v0, /device:TPU:24, one launch (start us, length us, event | category | flops | bytes accessed | tf_op | source)
XLA Modules:
  0.0 365.0 jit_solution(13443861393888478479)
XLA Ops:
  7.2 0.0 copy-start
  7.2 0.0 all-reduce.2.cloned.1.call-start
  7.2 1.2 copy-done
  8.4 0.0 copy-start.1
  8.4 3.3 multiply_convert_fusion
  11.7 0.0 copy-done.1
  11.7 0.8 convolution_bitcast_fusion
  12.5 0.0 copy-start.6
  12.5 2.9 copy.23
  15.5 0.0 copy-done.6
  15.5 0.0 copy-start.7
  15.5 0.0 copy-start.9
  15.5 2.2 fusion.5
  17.7 0.0 copy-start.11
  17.7 0.5 fusion.55
  18.3 10.3 %collective-permute-start.1 = (bf16[128,512]{1,0:T(8,128)(2,1)S(1)}, bf16[128,512]{1,0:T(8,128)(2,1)S(1)}, u32[]{:S(2)}, u32[]{:S(2)}) collective-permute-start(bf16[128,512]{1,0:T(8,128)(2,1)S(1)} %bitcast.132), channel_id=1, source_target_pairs={{1,0},{2,1},{3,2},{4,3},{5,4},{6,5},{7,6},{8,7},{9,8},{10,9},{11,1... | collective-permute-start | bytes 393224 | tf_op jit(solution)/shard_map/ppermute | solution.py:10
  28.6 0.0 copy-start.4
  28.6 0.0 copy-start.5
  28.6 2.1 collective-permute-start
  30.7 0.4 collective-permute-done.1
  31.1 6.1 %collective-permute-done = bf16[128,512]{1,0:T(8,128)(2,1)S(1)} collective-permute-done((bf16[128,512]{1,0:T(8,128)(2,1)S(1)}, bf16[128,512]{1,0:T(8,128)(2,1)S(1)}, u32[]{:S(2)}, u32[]{:S(2)}) %collective-permute-start) | collective-permute-done | bytes 131104 | tf_op jit(solution)/shard_map/ppermute | solution.py:10
  37.1 0.0 copy-done.7
  37.1 0.0 copy-done.9
  37.1 0.0 copy-start.10
  37.1 0.3 fusion.23
  37.4 1.9 collective-permute-start.3
  39.4 2.4 collective-permute-start.2
  41.8 0.0 copy-done.11
  41.8 0.1 collective-permute-done.3
  41.9 5.9 %collective-permute-done.2 = bf16[1,128,512]{2,1,0:T(8,128)(2,1)S(1)} collective-permute-done((bf16[1,128,512]{2,1,0:T(8,128)(2,1)S(1)}, bf16[1,128,512]{2,1,0:T(8,128)(2,1)S(1)}, u32[]{:S(2)}, u32[]{:S(2)}) %collective-permute-start.2) | collective-permute-done | bytes 131104 | tf_op jit(solution)/shard_map/ppermute | solution.py:21
  47.8 0.5 convolution_convert_fusion.2
  48.3 0.0 copy-done.4
  48.3 0.0 copy-done.5
  48.3 0.5 fusion.9
  48.9 0.0 copy-done.10
  48.9 0.6 convolution_bitcast_fusion.2
  49.5 0.2 copy.27
  49.7 0.6 fusion.47
  50.2 0.1 copy.61
  50.4 1.9 collective-permute-start.4
  52.3 5.8 %collective-permute-start.5 = (bf16[128,512]{1,0:T(8,128)(2,1)S(1)}, bf16[128,512]{1,0:T(8,128)(2,1)S(1)}, u32[]{:S(2)}, u32[]{:S(2)}) collective-permute-start(bf16[128,512]{1,0:T(8,128)(2,1)S(1)} %get-tuple-element.16), channel_id=1, source_target_pairs={{1,0},{2,1},{3,2},{4,3},{5,4},{6,5},{7,6},{8,7},{9,8},{10,9},{11,1... | collective-permute-start | bytes 393224 | tf_op jit(solution)/shard_map/ppermute | solution.py:10
  58.1 0.7 collective-permute-done.4
  58.8 1.8 collective-permute-done.5
  60.6 0.3 fusion.8
  60.9 0.0 copy-start.2
  60.9 6.0 %collective-permute-start.7 = (bf16[1,128,512]{2,1,0:T(8,128)(2,1)S(1)}, bf16[1,128,512]{2,1,0:T(8,128)(2,1)S(1)}, u32[]{:S(2)}, u32[]{:S(2)}) collective-permute-start(bf16[1,128,512]{2,1,0:T(8,128)(2,1)S(1)} %fusion.8), channel_id=1, source_target_pairs={{1,0},{2,1},{3,2},{4,3},{5,4},{6,5},{7,6},{8,7},{9,8},{10,9},{11,1... | collective-permute-start | bytes 393224 | tf_op jit(solution)/shard_map/ppermute | solution.py:23
  66.9 1.9 collective-permute-start.6
  68.8 0.6 collective-permute-done.7
  69.4 5.9 %collective-permute-done.6 = bf16[1,128,512]{2,1,0:T(8,128)(2,1)S(1)} collective-permute-done((bf16[1,128,512]{2,1,0:T(8,128)(2,1)S(1)}, bf16[1,128,512]{2,1,0:T(8,128)(2,1)S(1)}, u32[]{:S(2)}, u32[]{:S(2)}) %collective-permute-start.6) | collective-permute-done | bytes 131104 | tf_op jit(solution)/shard_map/ppermute | solution.py:21
  75.3 1.0 convolution_convert_fusion
  76.4 0.0 copy-done.2
  76.4 0.0 copy-start.3
  76.4 1.4 fusion.1
  77.8 0.2 copy-done.3
  78.0 0.8 fusion
  78.7 0.0 copy-start.8
  78.7 1.7 fusion.3
  80.5 0.0 all-reduce.2.cloned.1.call-update
  80.5 0.7 fusion.37
  81.2 0.0 copy-done.8
  81.2 1.7 fusion.4
  82.9 273.4 %all-reduce.2.cloned.1.call-done = f32[512,512]{0,1:T(8,128)} async-done(((f32[512,512]{0,1:T(8,128)}), f32[512,512]{0,1:T(8,128)}) %all-reduce.2.cloned.1.call-update) | async-done | bytes 1048592 | tf_op jit(solution)/shard_map/psum | solution.py:110
  356.3 1.1 constant_dynamic-slice_fusion
  357.4 0.7 copy.32
  (7 shorter events, 0.1 us)
Async XLA Ops:
  7.2 1.2 copy-start
  7.2 349.1 %all-reduce.2.cloned.1.call-start = ((), (), s32[]{:S(2)}) async-start(), calls=%async_computation | async-start | bytes 2097152 | tf_op jit(solution)/shard_map/psum | solution.py:110
  8.4 3.4 copy-start.1
  12.5 3.0 copy-start.6
  15.5 21.7 %copy-start.7 = (bf16[512,512]{1,0:T(8,128)(2,1)S(1)}, bf16[512,512]{1,0:T(8,128)(2,1)}, u32[]{:S(2)}) copy-start(bf16[512,512]{1,0:T(8,128)(2,1)} %param.18) | copy-start | bytes 1572868
  15.5 21.7 %copy-start.9 = (bf16[1,128,512]{2,1,0:T(8,128)(2,1)S(1)}, bf16[1,128,512]{2,1,0:T(8,128)(2,1)}, u32[]{:S(2)}) copy-start(bf16[1,128,512]{2,1,0:T(8,128)(2,1)} %param.11) | copy-start | bytes 393220
  17.7 24.1 %copy-start.11 = (s32[1,2]{1,0:T(1,128)S(1)}, s32[1,2]{1,0:T(1,128)}, u32[]{:S(2)}) copy-start(s32[1,2]{1,0:T(1,128)} %param.16) | copy-start | bytes 28
  18.3 12.8 %collective-permute-start.1 = (bf16[128,512]{1,0:T(8,128)(2,1)S(1)}, bf16[128,512]{1,0:T(8,128)(2,1)S(1)}, u32[]{:S(2)}, u32[]{:S(2)}) collective-permute-start(bf16[128,512]{1,0:T(8,128)(2,1)S(1)} %bitcast.132), channel_id=1, source_target_pairs={{1,0},{2,1},{3,2},{4,3},{5,4},{6,5},{7,6},{8,7},{9,8},{10,9},{11,1... | collective-permute-start | bytes 393224 | tf_op jit(solution)/shard_map/ppermute | solution.py:10
  28.6 19.7 %copy-start.4 = (bf16[512,512]{1,0:T(8,128)(2,1)S(1)}, bf16[512,512]{1,0:T(8,128)(2,1)}, u32[]{:S(2)}) copy-start(bf16[512,512]{1,0:T(8,128)(2,1)} %param.19) | copy-start | bytes 1572868
  28.6 19.7 %copy-start.5 = (bf16[1,2,128,128]{3,2,1,0:T(8,128)(2,1)S(1)}, bf16[1,2,128,128]{3,2,1,0:T(8,128)(2,1)}, u32[]{:S(2)}) copy-start(bf16[1,2,128,128]{3,2,1,0:T(8,128)(2,1)} %param.15) | copy-start | bytes 196612
  28.6 8.5 %collective-permute-start = (bf16[128,512]{1,0:T(8,128)(2,1)S(1)}, bf16[128,512]{1,0:T(8,128)(2,1)S(1)}, u32[]{:S(2)}, u32[]{:S(2)}) collective-permute-start(bf16[128,512]{1,0:T(8,128)(2,1)S(1)} %bitcast.133), channel_id=1, source_target_pairs={{0,1},{1,2},{2,3},{3,4},{4,5},{5,6},{6,7},{7,8},{8,9},{9,10},{10,1... | collective-permute-start | bytes 393224 | tf_op jit(solution)/shard_map/ppermute | solution.py:10
  37.1 11.7 %copy-start.10 = (bf16[1,128,512]{2,1,0:T(8,128)(2,1)S(1)}, bf16[1,128,512]{2,1,0:T(8,128)(2,1)}, u32[]{:S(2)}) copy-start(bf16[1,128,512]{2,1,0:T(8,128)(2,1)} %param.12) | copy-start | bytes 393220
  37.4 4.4 %collective-permute-start.3 = (bf16[1,128,512]{2,1,0:T(8,128)(2,1)S(1)}, bf16[1,128,512]{2,1,0:T(8,128)(2,1)S(1)}, u32[]{:S(2)}, u32[]{:S(2)}) collective-permute-start(bf16[1,128,512]{2,1,0:T(8,128)(2,1)S(1)} %bitcast.128), channel_id=1, source_target_pairs={{1,0},{2,1},{3,2},{4,3},{5,4},{6,5},{7,6},{8,7},{9,8},{10,9},{11,1... | collective-permute-start | bytes 393224 | tf_op jit(solution)/shard_map/ppermute | solution.py:23
  39.4 8.4 %collective-permute-start.2 = (bf16[1,128,512]{2,1,0:T(8,128)(2,1)S(1)}, bf16[1,128,512]{2,1,0:T(8,128)(2,1)S(1)}, u32[]{:S(2)}, u32[]{:S(2)}) collective-permute-start(bf16[1,128,512]{2,1,0:T(8,128)(2,1)S(1)} %bitcast.129), channel_id=1, source_target_pairs={{0,1},{1,2},{2,3},{3,4},{4,5},{5,6},{6,7},{7,8},{8,9},{9,10},{10,1... | collective-permute-start | bytes 393224 | tf_op jit(solution)/shard_map/ppermute | solution.py:21
  50.4 8.4 %collective-permute-start.4 = (bf16[128,512]{1,0:T(8,128)(2,1)S(1)}, bf16[128,512]{1,0:T(8,128)(2,1)S(1)}, u32[]{:S(2)}, u32[]{:S(2)}) collective-permute-start(bf16[128,512]{1,0:T(8,128)(2,1)S(1)} %get-tuple-element.15), channel_id=1, source_target_pairs={{0,1},{1,2},{2,3},{3,4},{4,5},{5,6},{6,7},{7,8},{8,9},{9,10},{10,1... | collective-permute-start | bytes 393224 | tf_op jit(solution)/shard_map/ppermute | solution.py:10
  52.3 8.3 %collective-permute-start.5 = (bf16[128,512]{1,0:T(8,128)(2,1)S(1)}, bf16[128,512]{1,0:T(8,128)(2,1)S(1)}, u32[]{:S(2)}, u32[]{:S(2)}) collective-permute-start(bf16[128,512]{1,0:T(8,128)(2,1)S(1)} %get-tuple-element.16), channel_id=1, source_target_pairs={{1,0},{2,1},{3,2},{4,3},{5,4},{6,5},{7,6},{8,7},{9,8},{10,9},{11,1... | collective-permute-start | bytes 393224 | tf_op jit(solution)/shard_map/ppermute | solution.py:10
  60.9 15.5 %copy-start.2 = (bf16[8,2,128,128]{3,2,1,0:T(8,128)(2,1)S(1)}, bf16[8,2,128,128]{3,2,1,0:T(8,128)(2,1)}, u32[]{:S(2)}) copy-start(bf16[8,2,128,128]{3,2,1,0:T(8,128)(2,1)} %param.13) | copy-start | bytes 1572868
  60.9 8.5 %collective-permute-start.7 = (bf16[1,128,512]{2,1,0:T(8,128)(2,1)S(1)}, bf16[1,128,512]{2,1,0:T(8,128)(2,1)S(1)}, u32[]{:S(2)}, u32[]{:S(2)}) collective-permute-start(bf16[1,128,512]{2,1,0:T(8,128)(2,1)S(1)} %fusion.8), channel_id=1, source_target_pairs={{1,0},{2,1},{3,2},{4,3},{5,4},{6,5},{7,6},{8,7},{9,8},{10,9},{11,1... | collective-permute-start | bytes 393224 | tf_op jit(solution)/shard_map/ppermute | solution.py:23
  66.9 8.4 %collective-permute-start.6 = (bf16[1,128,512]{2,1,0:T(8,128)(2,1)S(1)}, bf16[1,128,512]{2,1,0:T(8,128)(2,1)S(1)}, u32[]{:S(2)}, u32[]{:S(2)}) collective-permute-start(bf16[1,128,512]{2,1,0:T(8,128)(2,1)S(1)} %fusion.8), channel_id=1, source_target_pairs={{0,1},{1,2},{2,3},{3,4},{4,5},{5,6},{6,7},{7,8},{8,9},{9,10},{10,1... | collective-permute-start | bytes 393224 | tf_op jit(solution)/shard_map/ppermute | solution.py:21
  76.4 1.6 copy-start.3
  78.7 2.5 copy-start.8
Sparse Core Ops, SparseCore 0:
  80.6 275.6 all-reduce.1
where the time goes:
time: 365 us
  waiting for transfers between devices  295 us (81%)
  starting transfers between devices  32.3 us (9%)
  matrix products  14.9 us (4%)
  between operations  14.4 us (4%)
  local copies, waits for them, and re-layouts  6.5 us (2%)
    psum x1, waiting for transfers between devices, on_device(): summed = lax.psum(partial_grad, ('ens', 'grid'))  273 us
    ppermute x4, starting transfers between devices, passed_along(): lax.ppermute(value, axis, [(source, source + steps) for source in range(i...  20 us
    ppermute x2, waiting for transfers between devices, with_halo(): lax.ppermute(tail, axis, [(i, (i + 1) % count) for i in range(ends)])  11.8 us
    ppermute x4, waiting for transfers between devices, passed_along(): lax.ppermute(value, axis, [(source, source + steps) for source in range(i...  8.97 us
    ppermute x2, starting transfers between devices, with_halo(): lax.ppermute(head, axis, [((i + 1) % count, i) for i in range(ends)])  7.94 us
  transfers between devices with their start and end apart: 9, of which 9 were waited for; matrix products, arithmetic and copies ran while one was open for 1% of the time, Pallas kernels for 0%

commit v1 on v0

v1 whole, which is shorter than its diff:
```python
import jax
import jax.numpy as jnp
from jax import lax
from jax.sharding import Mesh
from jax.sharding import PartitionSpec as P

BF = jnp.bfloat16
F32 = jnp.float32
GRID = ("y", "z", "core")


def grid_split(count):
    cores = 2
    chips = count // cores
    ys = 1
    while ys * ys < chips:
        ys *= 2
    return ys, chips // ys, cores


def swap_pairs(count):
    mates = [(2 * c, 2 * c + 1) for c in range(count // 2)]
    across = [(2 * c + 1, 2 * c + 2) for c in range(count // 2 - 1)]
    both = lambda pairs: pairs + [(b, a) for a, b in pairs]
    return both(mates), both(across)


def dot(a, b, ca, cb):
    return lax.dot_general(a, b, (((ca,), (cb,)), ((), ())), preferred_element_type=F32)


def silu_slope(value):
    sig = jax.nn.sigmoid(value)
    return sig * (1.0 + value * (1.0 - sig))


def spread(weights, slots):
    blocks, picks, rows, cols = weights.shape
    three = jnp.arange(3, dtype=jnp.int32)
    hit = slots[:, :, None] == three
    laid = sum(
        jnp.where(hit[:, k, :, None, None], weights[:, k, None], jnp.zeros((), BF))
        for k in range(picks)
    )
    return laid.transpose(1, 2, 0, 3).reshape(3 * rows, blocks * cols)


def on_device(
    grid_latent, mesh_latent, cotangent, edge_weights, edge_targets,
    mesh_weights, mesh_sources, encode_weight, aggregate_weight, process_weight,
):
    members = lax.axis_size("ens")
    bands = lax.axis_size(GRID)
    here = lax.axis_index(GRID)
    core = lax.axis_index("core")
    sign = 1 - 2 * core
    mates, across = swap_pairs(bands)
    blocks, _, rows, _ = edge_weights.shape
    width = grid_latent.shape[2]
    half = width // 2

    def exchange(to_across, to_mate):
        from_across = lax.ppermute(to_across, GRID, across)
        from_mate = lax.ppermute(to_mate, GRID, mates)
        return from_across, from_mate

    edge_slots = (edge_targets - here) * sign + 1
    mesh_slots = (mesh_sources - here) * sign + 1
    edges = spread(edge_weights, edge_slots)
    grid_x = grid_latent[0]
    encoded = dot(grid_x, encode_weight, 1, 0)
    messages = jax.nn.silu(encoded).astype(BF)
    panels = dot(edges, messages, 1, 0).astype(BF)
    a, m = exchange(panels[:rows], panels[2 * rows :])
    aggregated = (
        panels[rows : 2 * rows].astype(F32) + a.astype(F32) + m.astype(F32)
    ).astype(BF)
    mesh_pre = dot(aggregated, aggregate_weight, 1, 0)
    updated = (mesh_latent[0].astype(F32) + jax.nn.silu(mesh_pre)).astype(BF)
    a, m = exchange(updated, updated)
    nearby = jnp.concatenate([a, updated, m], 0)
    mixing = spread(mesh_weights[0][None].transpose(0, 1, 3, 2), mesh_slots)
    processed = dot(mixing, nearby, 0, 0).astype(BF)
    proc_pre = dot(processed, process_weight, 1, 0)
    result = (updated.astype(F32) + jax.nn.silu(proc_pre)).astype(BF)
    upstream = cotangent[0].astype(F32)
    proc_delta = (upstream * silu_slope(proc_pre)).astype(BF)
    proc_back = dot(proc_delta, process_weight, 1, 1).astype(BF)
    pushed = dot(mixing, proc_back, 1, 0).astype(BF)
    a, m = exchange(pushed[:rows], pushed[2 * rows :])
    mesh_grad = upstream + pushed[rows : 2 * rows].astype(F32) + a.astype(F32) + m.astype(F32)
    mesh_delta = (mesh_grad * silu_slope(mesh_pre)).astype(BF)
    agg_grad = dot(mesh_delta, aggregate_weight, 1, 1).astype(BF)
    a, m = exchange(agg_grad, agg_grad)
    returned = jnp.concatenate([a, agg_grad, m], 0)
    message_grad = dot(edges, returned, 0, 0)
    enc_delta = (message_grad * silu_slope(encoded)).astype(BF)
    theirs = lax.dynamic_slice_in_dim(enc_delta, (1 - core) * half, half, 1)
    ours = lax.dynamic_slice_in_dim(enc_delta, core * half, half, 1)
    arrived = lax.ppermute(dot(grid_x, theirs, 0, 0).astype(BF), GRID, mates)
    grid_grad = dot(enc_delta, encode_weight, 1, 1).astype(BF)
    pair = (dot(grid_x, ours, 0, 0) + arrived.astype(F32)).astype(BF)
    chips = bands // 2
    share = width // chips
    parts = lax.all_to_all(pair.reshape(chips, share, half), ("y", "z"), 0, 0)
    column = parts.astype(F32).sum(0)
    scale = 1.0 / float(members * blocks * rows * bands) ** 0.5
    column = (column * scale).reshape(1, 2, share // 2, half)
    column = jnp.broadcast_to(column, (members,) + column.shape[1:])
    column = column.reshape(members * 2, share // 2, half)
    last = lax.all_to_all(column, ("ens", "core"), 0, 0)
    last = last.reshape(members, 2, share // 2, half).sum(0)
    final = last.transpose(1, 0, 2).reshape(share // 2, width)
    return result[None], grid_grad[None], final


def solution(mesh):
    ens, bands = mesh.devices.shape
    fine = Mesh(mesh.devices.reshape((ens,) + grid_split(bands)), ("ens",) + GRID)
    return jax.shard_map(
        on_device,
        mesh=fine,
        in_specs=(
            P("ens", GRID, None),
            P("ens", GRID, None),
            P("ens", GRID, None),
            P(GRID, None, None, None),
            P(GRID, None),
            P(GRID, None, None, None),
            P(GRID, None),
            P(),
            P(),
            P(),
        ),
        out_specs=(P("ens", GRID, None), P("ens", GRID, None), P(GRID, None)),
        check_vma=False,
    )
```

time: 365 us -> 113 us (0.31)
  the two profiles are of different devices: /device:TPU:24 before, /device:TPU:1 now
where the time goes in v1:
time: 113 us; the launch traced here: 112 us
  starting transfers between devices  56.2 us (50%)
  waiting for transfers between devices  25.9 us (23%)
  matrix products  16.6 us (15%)
  local copies, waits for them, and re-layouts  9.92 us (9%)
  other arithmetic  2.65 us (2%)
    all_to_all x1, starting transfers between devices, on_device(): parts = lax.all_to_all(pair.reshape(chips, share, half), ('y', 'z'), 0, 0)  22 us
    dot_general x10, matrix products, dot(): lax.dot_general(a, b, (((ca,), (cb,)), ((), ())), preferred_element_type=...  16.6 us
    ppermute x4, starting transfers between devices, exchange(): from_mate = lax.ppermute(to_mate, GRID, mates)  14.5 us
    all_to_all x1, waiting for transfers between devices, on_device(): parts = lax.all_to_all(pair.reshape(chips, share, half), ('y', 'z'), 0, 0)  12.6 us
    ppermute x4, starting transfers between devices, exchange(): from_across = lax.ppermute(to_across, GRID, across)  11 us
    ppermute x4, waiting for transfers between devices, exchange(): from_across = lax.ppermute(to_across, GRID, across)  10 us
    all_to_all x1, starting transfers between devices, on_device(): last = lax.all_to_all(column, ('ens', 'core'), 0, 0)  6.65 us
    broadcast_in_dim x9, local copies, waits for them, and re-layouts, spread(): jnp.where(hit[:, k, :, None, None], weights[:, k, None], jnp.zeros((), BF))  5.06 us
  transfers between devices with their start and end apart: 11, of which 7 were waited for; matrix products, arithmetic and copies ran while one was open for 7% of the time, Pallas kernels for 0%

profile of v1, /device:TPU:1, one launch (start us, length us, event | category | flops | bytes accessed | tf_op | source)
XLA Modules:
  0.0 112.3 jit_solution(13543197575253287200)
XLA Ops:
  0.6 0.0 copy-start
  0.7 0.0 copy-start.2
  0.7 0.8 multiply_add_fusion
  1.5 1.1 slice_bitcast_fusion.1
  2.6 0.2 copy.23
  2.7 0.2 copy.22
  2.9 0.0 copy-done
  2.9 0.0 copy-done.2
  2.9 0.7 fusion.5
  3.6 0.2 select_add_fusion
  3.8 0.0 copy-start.1
  3.8 0.0 copy-start.9
  3.8 0.0 copy-start.8
  3.9 0.9 convolution_convert_fusion.2
  4.7 0.0 copy-done.1
  4.8 0.7 fusion.62
  5.5 8.8 %collective-permute-start.1 = (bf16[128,512]{1,0:T(8,128)(2,1)}, bf16[128,512]{1,0:T(8,128)(2,1)}, u32[]{:S(2)}, u32[]{:S(2)}) collective-permute-start(bf16[128,512]{1,0:T(8,128)(2,1)} %get-tuple-element.8), channel_id=1, source_target_pairs={{0,1},{2,3},{4,5},{6,7},{8,9},{10,11},{12,13},{14,15},{16,17},{18,... | collective-permute-start | bytes 393224 | tf_op jit(solution)/shard_map/ppermute | solution.py:64
  14.2 1.9 %collective-permute-start = (bf16[128,512]{1,0:T(8,128)(2,1)}, bf16[128,512]{1,0:T(8,128)(2,1)}, u32[]{:S(2)}, u32[]{:S(2)}) collective-permute-start(bf16[128,512]{1,0:T(8,128)(2,1)} %get-tuple-element.7), channel_id=1, source_target_pairs={{1,2},{3,4},{5,6},{7,8},{9,10},{11,12},{13,14},{15,16},{17,18},{19... | collective-permute-start | bytes 393224 | tf_op jit(solution)/shard_map/ppermute | solution.py:63
  16.2 0.0 copy-done.9
  16.2 0.1 iota_compare_fusion.1
  16.3 0.0 copy-done.8
  16.3 0.6 slice_bitcast_fusion.3
  16.9 1.5 %copy.25 = bf16[128,128]{1,0:T(8,128)(2,1)} copy(bf16[128,128]{0,1:T(8,128)(2,1)} %get-tuple-element.10) | data formatting | bytes 65536 | tf_op jit(solution)/shard_map/jit(_where)/broadcast_in_dim | solution.py:42
  18.4 1.5 %copy.24 = bf16[128,128]{1,0:T(8,128)(2,1)} copy(bf16[128,128]{0,1:T(8,128)(2,1)} %get-tuple-element.9) | data formatting | bytes 65536 | tf_op jit(solution)/shard_map/jit(_where)/broadcast_in_dim | solution.py:42
  19.8 0.0 collective-permute-done.1
  19.8 1.0 collective-permute-done
  20.8 2.1 %fusion.37 = (bf16[128,512]{1,0:T(8,128)(2,1)S(1)}, f32[128,512]{1,0:T(8,128)}) fusion(bf16[1,128,512]{2,1,0:T(8,128)(2,1)} %param.11, bf16[512,512]{1,0:T(8,128)(2,1)} %param.18, bf16[128,512]{1,0:T(8,128)(2,1)} %collective-permute-done.1, bf16[128,512]{1,0:T(8,128)(2,1)} %collective-permute-done, bf16[384,512]{1,0:T(8,128)(2,1)S(1)} %convolution_convert_fusion.2), kind=kOutput, calls=%fused_computation.45 | convolution fusion | flops 67960832 | bytes 1441792 | tf_op jit(solution)/shard_map/dot_general | solution.py:29
  23.0 1.9 %collective-permute-start.3 = (bf16[128,512]{1,0:T(8,128)(2,1)S(1)}, bf16[128,512]{1,0:T(8,128)(2,1)S(1)}, u32[]{:S(2)}, u32[]{:S(2)}) collective-permute-start(bf16[128,512]{1,0:T(8,128)(2,1)S(1)} %get-tuple-element.15), channel_id=1, source_target_pairs={{0,1},{2,3},{4,5},{6,7},{8,9},{10,11},{12,13},{14,15},{16,17},{18,... | collective-permute-start | bytes 393224 | tf_op jit(solution)/shard_map/ppermute | solution.py:64
  24.9 2.7 %collective-permute-start.2 = (bf16[128,512]{1,0:T(8,128)(2,1)S(1)}, bf16[128,512]{1,0:T(8,128)(2,1)}, u32[]{:S(2)}, u32[]{:S(2)}) collective-permute-start(bf16[128,512]{1,0:T(8,128)(2,1)S(1)} %get-tuple-element.15), channel_id=1, source_target_pairs={{1,2},{3,4},{5,6},{7,8},{9,10},{11,12},{13,14},{15,16},{17,18},{19... | collective-permute-start | bytes 393224 | tf_op jit(solution)/shard_map/ppermute | solution.py:63
  27.6 0.1 broadcast_bitcast_fusion
  27.6 0.2 fusion.51
  27.8 0.0 collective-permute-done.3
  27.8 0.0 copy-start.10
  27.8 0.6 copy-done.10
  28.5 2.8 %collective-permute-done.2 = bf16[128,512]{1,0:T(8,128)(2,1)} collective-permute-done((bf16[128,512]{1,0:T(8,128)(2,1)S(1)}, bf16[128,512]{1,0:T(8,128)(2,1)}, u32[]{:S(2)}, u32[]{:S(2)}) %collective-permute-start.2) | collective-permute-done | bytes 131104 | tf_op jit(solution)/shard_map/ppermute | solution.py:63
  31.3 1.6 %fusion.2 = f32[128,512]{1,0:T(8,128)S(1)} fusion(bf16[512,512]{1,0:T(8,128)(2,1)} %param.19, bf16[384,128]{1,0:T(8,128)(2,1)S(1)} %fusion.51, bf16[128,512]{1,0:T(8,128)(2,1)} %copy-done.10, bf16[128,512]{1,0:T(8,128)(2,1)} %copy-done.6, bf16[128,512]{1,0:T(8,128)(2,1)} %collective-permute-done.2), kind=kOutput, calls=%fused_computation.13 | convolution fusion | flops 118685696 | bytes 1277952 | tf_op jit(solution)/shard_map/dot_general | solution.py:29
  32.9 2.4 %convolution_convert_fusion.1 = bf16[384,512]{1,0:T(8,128)(2,1)} fusion(bf16[384,128]{1,0:T(8,128)(2,1)S(1)} %fusion.51, bf16[512,512]{1,0:T(8,128)(2,1)} %param.19, f32[128,512]{1,0:T(8,128)S(1)} %fusion.2, bf16[1,128,512]{2,1,0:T(8,128)(2,1)} %param.12), kind=kOutput, calls=%fused_computation.5 | convolution fusion | flops 118358016 | bytes 1409024 | tf_op jit(solution)/shard_map/dot_general | solution.py:29
  35.3 1.0 fusion.61
  36.3 1.9 %collective-permute-start.5 = (bf16[128,512]{1,0:T(8,128)(2,1)S(1)}, bf16[128,512]{1,0:T(8,128)(2,1)S(1)}, u32[]{:S(2)}, u32[]{:S(2)}) collective-permute-start(bf16[128,512]{1,0:T(8,128)(2,1)S(1)} %get-tuple-element.6), channel_id=1, source_target_pairs={{0,1},{2,3},{4,5},{6,7},{8,9},{10,11},{12,13},{14,15},{16,17},{18,... | collective-permute-start | bytes 393224 | tf_op jit(solution)/shard_map/ppermute | solution.py:64
  38.2 3.1 %collective-permute-start.4 = (bf16[128,512]{1,0:T(8,128)(2,1)S(1)}, bf16[128,512]{1,0:T(8,128)(2,1)S(1)}, u32[]{:S(2)}, u32[]{:S(2)}) collective-permute-start(bf16[128,512]{1,0:T(8,128)(2,1)S(1)} %get-tuple-element.5), channel_id=1, source_target_pairs={{1,2},{3,4},{5,6},{7,8},{9,10},{11,12},{13,14},{15,16},{17,18},{19... | collective-permute-start | bytes 393224 | tf_op jit(solution)/shard_map/ppermute | solution.py:63
  41.4 0.0 collective-permute-done.5
  41.4 3.1 %collective-permute-done.4 = bf16[128,512]{1,0:T(8,128)(2,1)S(1)} collective-permute-done((bf16[128,512]{1,0:T(8,128)(2,1)S(1)}, bf16[128,512]{1,0:T(8,128)(2,1)S(1)}, u32[]{:S(2)}, u32[]{:S(2)}) %collective-permute-start.4) | collective-permute-done | bytes 131104 | tf_op jit(solution)/shard_map/ppermute | solution.py:63
  44.5 1.6 %convolution_convert_fusion.4 = bf16[128,512]{1,0:T(8,128)(2,1)S(1)} fusion(bf16[512,512]{1,0:T(8,128)(2,1)} %param.18, f32[128,512]{1,0:T(8,128)} %get-tuple-element.16, bf16[128,512]{1,0:T(8,128)(2,1)S(1)} %collective-permute-done.5, bf16[128,512]{1,0:T(8,128)(2,1)S(1)} %collective-permute-done.4, bf16[384,512]{1,0:T(8,128)(2,1)} %convolution_convert_fusion.1, ...), kind=kOutput, calls=%fused_computation.10 | convolution fusion | flops 68222976 | bytes 1441792 | tf_op jit(solution)/shard_map/dot_general | solution.py:29
  46.1 1.9 %collective-permute-start.7 = (bf16[128,512]{1,0:T(8,128)(2,1)S(1)}, bf16[128,512]{1,0:T(8,128)(2,1)}, u32[]{:S(2)}, u32[]{:S(2)}) collective-permute-start(bf16[128,512]{1,0:T(8,128)(2,1)S(1)} %convolution_convert_fusion.4), channel_id=1, source_target_pairs={{0,1},{2,3},{4,5},{6,7},{8,9},{10,11},{12,13},{14,15},{16,17},{18,... | collective-permute-start | bytes 393224 | tf_op jit(solution)/shard_map/ppermute | solution.py:64
  48.0 3.3 %collective-permute-start.6 = (bf16[128,512]{1,0:T(8,128)(2,1)S(1)}, bf16[128,512]{1,0:T(8,128)(2,1)}, u32[]{:S(2)}, u32[]{:S(2)}) collective-permute-start(bf16[128,512]{1,0:T(8,128)(2,1)S(1)} %convolution_convert_fusion.4), channel_id=1, source_target_pairs={{1,2},{3,4},{5,6},{7,8},{9,10},{11,12},{13,14},{15,16},{17,18},{19... | collective-permute-start | bytes 393224 | tf_op jit(solution)/shard_map/ppermute | solution.py:63
  51.3 0.0 collective-permute-done.7
  51.3 3.1 %collective-permute-done.6 = bf16[128,512]{1,0:T(8,128)(2,1)} collective-permute-done((bf16[128,512]{1,0:T(8,128)(2,1)S(1)}, bf16[128,512]{1,0:T(8,128)(2,1)}, u32[]{:S(2)}, u32[]{:S(2)}) %collective-permute-start.6) | collective-permute-done | bytes 131104 | tf_op jit(solution)/shard_map/ppermute | solution.py:63
  54.4 2.4 %multiply_convert_fusion = bf16[1024,512]{1,0:T(8,128)(2,1)S(1)} fusion(f32[1024,512]{1,0:T(8,128)S(1)} %fusion.5, bf16[48,8,8,128]{3,2,1,0:T(8,128)(2,1)} %bitcast.95, bf16[128,512]{1,0:T(8,128)(2,1)} %collective-permute-done.7, bf16[128,512]{1,0:T(8,128)(2,1)S(1)} %convolution_convert_fusion.4, bf16[128,512]{1,0:T(8,128)(2,1)} %collective-permute-done.6), kind=kOutput, calls=%fused_computation | convolution fusion | flops 408551424 | bytes 4325376 | tf_op jit(solution)/shard_map/dot_general | solution.py:29
  56.8 1.0 copy-done.11
  57.8 0.5 fusion.1
  58.3 2.1 %collective-permute-start.8 = (bf16[512,256]{0,1:T(8,128)(2,1)S(1)}, bf16[512,256]{0,1:T(8,128)(2,1)S(1)}, u32[]{:S(2)}, u32[]{:S(2)}) collective-permute-start(bf16[512,256]{0,1:T(8,128)(2,1)S(1)} %fusion.1), channel_id=1, source_target_pairs={{0,1},{2,3},{4,5},{6,7},{8,9},{10,11},{12,13},{14,15},{16,17},{18,... | collective-permute-start | bytes 786440 | tf_op jit(solution)/shard_map/ppermute | solution.py:100
  60.4 0.0 copy-start.3
  60.4 1.5 %collective-permute-done.8 = bf16[512,256]{0,1:T(8,128)(2,1)S(1)} collective-permute-done((bf16[512,256]{0,1:T(8,128)(2,1)S(1)}, bf16[512,256]{0,1:T(8,128)(2,1)S(1)}, u32[]{:S(2)}, u32[]{:S(2)}) %collective-permute-start.8) | collective-permute-done | bytes 262176 | tf_op jit(solution)/shard_map/ppermute | solution.py:100
  61.9 1.5 %add_convert_fusion = bf16[512,256]{0,1:T(8,128)(2,1)S(1)} fusion(bf16[512,256]{0,1:T(8,128)(2,1)S(1)} %collective-permute-done.8, bf16[1,1024,512]{2,1,0:T(8,128)(2,1)S(1)} %copy-done, bf16[1024,512]{1,0:T(8,128)(2,1)} %copy-done.11, s32[]{:T(128)S(6)} %select_n.36), kind=kOutput, calls=%fused_computation.24 | convolution fusion | flops 268828672 | bytes 2097156 | tf_op jit(solution)/shard_map/dot_general | solution.py:29
  63.4 0.8 copy.26
  64.2 22.0 %all-to-all-start = ((bf16[64,8,256]{2,1,0:T(8,128)(2,1)}), bf16[64,8,256]{2,1,0:T(8,128)(2,1)S(1)}, u32[]{:S(2)}, u32[]{:S(2)}) async-start(bf16[64,8,256]{2,1,0:T(8,128)(2,1)} %bitcast.26), calls=%async_computation | async-start | bytes 524288 | tf_op jit(solution)/shard_map/all_to_all | solution.py:105
  86.2 0.7 fusion.50
  87.0 12.6 %all-to-all-done = bf16[64,8,256]{2,1,0:T(8,128)(2,1)S(1)} async-done(((bf16[64,8,256]{2,1,0:T(8,128)(2,1)}), bf16[64,8,256]{2,1,0:T(8,128)(2,1)S(1)}, u32[]{:S(2)}, u32[]{:S(2)}) %all-to-all-start) | async-done | bytes 262176 | tf_op jit(solution)/shard_map/all_to_all | solution.py:105
  99.6 0.1 convert_reduce_fusion
  99.7 0.6 broadcast_in_dim.143
  100.3 6.6 %all-to-all-start.1 = ((f32[8,4,256]{2,1,0:T(4,128)}), f32[8,4,256]{2,1,0:T(4,128)S(1)}, u32[]{:S(2)}, u32[]{:S(2)}) async-start(f32[8,4,256]{2,1,0:T(4,128)} %bitcast.27), calls=%async_computation.1 | async-start | bytes 65536 | tf_op jit(solution)/shard_map/all_to_all | solution.py:111
  107.0 2.9 %fusion = bf16[1,1024,512]{2,1,0:T(8,128)(2,1)} fusion(bf16[1024,512]{1,0:T(8,128)(2,1)} %copy-done.11, bf16[512,512]{1,0:T(8,128)(2,1)S(1)} %copy-done.3), kind=kOutput, calls=%fused_computation.4 | convolution fusion | flops 537395200 | bytes 2621440 | tf_op jit(solution)/shard_map/dot_general | solution.py:29
  109.9 1.8 %all-to-all-done.1 = f32[8,4,256]{2,1,0:T(4,128)S(1)} async-done(((f32[8,4,256]{2,1,0:T(4,128)}), f32[8,4,256]{2,1,0:T(4,128)S(1)}, u32[]{:S(2)}, u32[]{:S(2)}) %all-to-all-start.1) | async-done | bytes 32800 | tf_op jit(solution)/shard_map/all_to_all | solution.py:111
  111.7 0.6 reduce_sum.19
  (16 shorter events, 0.1 us)
Async XLA Ops:
  0.6 2.3 %copy-start = (bf16[1,1024,512]{2,1,0:T(8,128)(2,1)S(1)}, bf16[1,1024,512]{2,1,0:T(8,128)(2,1)}, u32[]{:S(2)}) copy-start(bf16[1,1024,512]{2,1,0:T(8,128)(2,1)} %param.10) | copy-start | bytes 3145732
  0.7 2.3 %copy-start.2 = (bf16[512,512]{1,0:T(8,128)(2,1)S(1)}, bf16[512,512]{1,0:T(8,128)(2,1)}, u32[]{:S(2)}) copy-start(bf16[512,512]{1,0:T(8,128)(2,1)} %param.17) | copy-start | bytes 1572868
  3.8 0.9 copy-start.1
  3.8 12.3 %copy-start.9 = (s32[1,2]{1,0:T(1,128)S(1)}, s32[1,2]{1,0:T(1,128)}, u32[]{:S(2)}) copy-start(s32[1,2]{1,0:T(1,128)} %param.16) | copy-start | bytes 28
  3.8 12.4 %copy-start.8 = (bf16[1,2,128,128]{3,2,1,0:T(8,128)(2,1)S(1)}, bf16[1,2,128,128]{3,2,1,0:T(8,128)(2,1)}, u32[]{:S(2)}) copy-start(bf16[1,2,128,128]{3,2,1,0:T(8,128)(2,1)} %param.15) | copy-start | bytes 196612
  5.5 14.4 %collective-permute-start.1 = (bf16[128,512]{1,0:T(8,128)(2,1)}, bf16[128,512]{1,0:T(8,128)(2,1)}, u32[]{:S(2)}, u32[]{:S(2)}) collective-permute-start(bf16[128,512]{1,0:T(8,128)(2,1)} %get-tuple-element.8), channel_id=1, source_target_pairs={{0,1},{2,3},{4,5},{6,7},{8,9},{10,11},{12,13},{14,15},{16,17},{18,... | collective-permute-start | bytes 393224 | tf_op jit(solution)/shard_map/ppermute | solution.py:64
  14.2 6.6 %collective-permute-start = (bf16[128,512]{1,0:T(8,128)(2,1)}, bf16[128,512]{1,0:T(8,128)(2,1)}, u32[]{:S(2)}, u32[]{:S(2)}) collective-permute-start(bf16[128,512]{1,0:T(8,128)(2,1)} %get-tuple-element.7), channel_id=1, source_target_pairs={{1,2},{3,4},{5,6},{7,8},{9,10},{11,12},{13,14},{15,16},{17,18},{19... | collective-permute-start | bytes 393224 | tf_op jit(solution)/shard_map/ppermute | solution.py:63
  19.8 7.8 %copy-start.4 = (bf16[128,128]{1,0:T(8,128)(2,1)S(1)}, bf16[128,128]{1,0:T(8,128)(2,1)}, u32[]{:S(2)}) copy-start(bf16[128,128]{1,0:T(8,128)(2,1)} %copy.25) | copy-start | bytes 98308
  19.8 7.8 %copy-start.5 = (bf16[128,128]{1,0:T(8,128)(2,1)S(1)}, bf16[128,128]{1,0:T(8,128)(2,1)}, u32[]{:S(2)}) copy-start(bf16[128,128]{1,0:T(8,128)(2,1)} %copy.24) | copy-start | bytes 98308
  23.0 4.9 %copy-start.6 = (bf16[128,512]{1,0:T(8,128)(2,1)}, bf16[128,512]{1,0:T(8,128)(2,1)S(1)}, u32[]{:S(2)}) copy-start(bf16[128,512]{1,0:T(8,128)(2,1)S(1)} %get-tuple-element.15) | copy-start | bytes 393220
  23.0 4.8 %collective-permute-start.3 = (bf16[128,512]{1,0:T(8,128)(2,1)S(1)}, bf16[128,512]{1,0:T(8,128)(2,1)S(1)}, u32[]{:S(2)}, u32[]{:S(2)}) collective-permute-start(bf16[128,512]{1,0:T(8,128)(2,1)S(1)} %get-tuple-element.15), channel_id=1, source_target_pairs={{0,1},{2,3},{4,5},{6,7},{8,9},{10,11},{12,13},{14,15},{16,17},{18,... | collective-permute-start | bytes 393224 | tf_op jit(solution)/shard_map/ppermute | solution.py:64
  24.9 6.4 %collective-permute-start.2 = (bf16[128,512]{1,0:T(8,128)(2,1)S(1)}, bf16[128,512]{1,0:T(8,128)(2,1)}, u32[]{:S(2)}, u32[]{:S(2)}) collective-permute-start(bf16[128,512]{1,0:T(8,128)(2,1)S(1)} %get-tuple-element.15), channel_id=1, source_target_pairs={{1,2},{3,4},{5,6},{7,8},{9,10},{11,12},{13,14},{15,16},{17,18},{19... | collective-permute-start | bytes 393224 | tf_op jit(solution)/shard_map/ppermute | solution.py:63
  27.8 0.7 copy-start.10
  36.3 5.1 %collective-permute-start.5 = (bf16[128,512]{1,0:T(8,128)(2,1)S(1)}, bf16[128,512]{1,0:T(8,128)(2,1)S(1)}, u32[]{:S(2)}, u32[]{:S(2)}) collective-permute-start(bf16[128,512]{1,0:T(8,128)(2,1)S(1)} %get-tuple-element.6), channel_id=1, source_target_pairs={{0,1},{2,3},{4,5},{6,7},{8,9},{10,11},{12,13},{14,15},{16,17},{18,... | collective-permute-start | bytes 393224 | tf_op jit(solution)/shard_map/ppermute | solution.py:64
  38.2 6.3 %collective-permute-start.4 = (bf16[128,512]{1,0:T(8,128)(2,1)S(1)}, bf16[128,512]{1,0:T(8,128)(2,1)S(1)}, u32[]{:S(2)}, u32[]{:S(2)}) collective-permute-start(bf16[128,512]{1,0:T(8,128)(2,1)S(1)} %get-tuple-element.5), channel_id=1, source_target_pairs={{1,2},{3,4},{5,6},{7,8},{9,10},{11,12},{13,14},{15,16},{17,18},{19... | collective-permute-start | bytes 393224 | tf_op jit(solution)/shard_map/ppermute | solution.py:63
  46.1 5.2 %collective-permute-start.7 = (bf16[128,512]{1,0:T(8,128)(2,1)S(1)}, bf16[128,512]{1,0:T(8,128)(2,1)}, u32[]{:S(2)}, u32[]{:S(2)}) collective-permute-start(bf16[128,512]{1,0:T(8,128)(2,1)S(1)} %convolution_convert_fusion.4), channel_id=1, source_target_pairs={{0,1},{2,3},{4,5},{6,7},{8,9},{10,11},{12,13},{14,15},{16,17},{18,... | collective-permute-start | bytes 393224 | tf_op jit(solution)/shard_map/ppermute | solution.py:64
  48.0 6.4 %collective-permute-start.6 = (bf16[128,512]{1,0:T(8,128)(2,1)S(1)}, bf16[128,512]{1,0:T(8,128)(2,1)}, u32[]{:S(2)}, u32[]{:S(2)}) collective-permute-start(bf16[128,512]{1,0:T(8,128)(2,1)S(1)} %convolution_convert_fusion.4), channel_id=1, source_target_pairs={{1,2},{3,4},{5,6},{7,8},{9,10},{11,12},{13,14},{15,16},{17,18},{19... | collective-permute-start | bytes 393224 | tf_op jit(solution)/shard_map/ppermute | solution.py:63
  56.8 1.0 copy-start.11
  58.3 27.9 %copy-start.7 = (bf16[128,512]{1,0:T(8,128)(2,1)S(1)}, bf16[128,512]{1,0:T(8,128)(2,1)}, u32[]{:S(2)}) copy-start(bf16[128,512]{1,0:T(8,128)(2,1)} %copy-done.6) | copy-start | bytes 393220
  58.3 3.6 %collective-permute-start.8 = (bf16[512,256]{0,1:T(8,128)(2,1)S(1)}, bf16[512,256]{0,1:T(8,128)(2,1)S(1)}, u32[]{:S(2)}, u32[]{:S(2)}) collective-permute-start(bf16[512,256]{0,1:T(8,128)(2,1)S(1)} %fusion.1), channel_id=1, source_target_pairs={{0,1},{2,3},{4,5},{6,7},{8,9},{10,11},{12,13},{14,15},{16,17},{18,... | collective-permute-start | bytes 786440 | tf_op jit(solution)/shard_map/ppermute | solution.py:100
  60.4 46.6 %copy-start.3 = (bf16[512,512]{1,0:T(8,128)(2,1)S(1)}, bf16[512,512]{1,0:T(8,128)(2,1)}, u32[]{:S(2)}) copy-start(bf16[512,512]{1,0:T(8,128)(2,1)} %param.17) | copy-start | bytes 1572868
  64.2 35.4 %all-to-all-start = ((bf16[64,8,256]{2,1,0:T(8,128)(2,1)}), bf16[64,8,256]{2,1,0:T(8,128)(2,1)S(1)}, u32[]{:S(2)}, u32[]{:S(2)}) async-start(bf16[64,8,256]{2,1,0:T(8,128)(2,1)} %bitcast.26), calls=%async_computation | async-start | bytes 524288 | tf_op jit(solution)/shard_map/all_to_all | solution.py:105
  100.3 11.4 %all-to-all-start.1 = ((f32[8,4,256]{2,1,0:T(4,128)}), f32[8,4,256]{2,1,0:T(4,128)S(1)}, u32[]{:S(2)}, u32[]{:S(2)}) async-start(f32[8,4,256]{2,1,0:T(4,128)} %bitcast.27), calls=%async_computation.1 | async-start | bytes 65536 | tf_op jit(solution)/shard_map/all_to_all | solution.py:111

commit v2 on v1

v2 whole, which is shorter than its diff:
```python
import functools

import jax
import jax.numpy as jnp
from jax import lax
from jax.experimental import pallas as pl
from jax.experimental.pallas import tpu as pltpu
from jax.sharding import Mesh
from jax.sharding import PartitionSpec as P

BF = jnp.bfloat16
F32 = jnp.float32
GRID = ("y", "z", "core")


def grid_split(count):
    cores = 2
    chips = count // cores
    ys = 1
    while ys * ys < chips:
        ys *= 2
    return ys, chips // ys, cores


def swap_pairs(count):
    mates = [(2 * c, 2 * c + 1) for c in range(count // 2)]
    across = [(2 * c + 1, 2 * c + 2) for c in range(count // 2 - 1)]
    both = lambda pairs: pairs + [(b, a) for a, b in pairs]
    return both(mates), both(across)


def dot(a, b, ca, cb):
    return lax.dot_general(a, b, (((ca,), (cb,)), ((), ())), preferred_element_type=F32)


def sigmoid(value):
    return 0.5 * jnp.tanh(0.5 * value) + 0.5


def silu_and_slope(value):
    sig = sigmoid(value)
    lifted = value * sig
    return lifted, sig + lifted - lifted * sig


def call(kernel, outs, scratch, flops, moved, *operands, copied=False):
    floats = pltpu.HBM if copied else pltpu.VMEM
    specs = [
        pl.BlockSpec(memory_space=pltpu.SMEM if o.dtype == jnp.int32 else floats)
        for o in operands
    ]
    single = len(outs) == 1
    shapes = [jax.ShapeDtypeStruct(shape, kind) for shape, kind in outs]
    vmem = [pl.BlockSpec(memory_space=pltpu.VMEM) for _ in outs]
    return pl.pallas_call(
        kernel,
        out_shape=shapes[0] if single else shapes,
        in_specs=specs,
        out_specs=vmem[0] if single else vmem,
        scratch_shapes=[pltpu.VMEM(*o) if isinstance(o, tuple) else o for o in scratch],
        compiler_params=pltpu.CompilerParams(vmem_limit_bytes=(60 if copied else 24) << 20),
        cost_estimate=pl.CostEstimate(flops=flops, bytes_accessed=moved, transcendentals=0),
    )(*operands)


def slot_of(block):
    here = lax.axis_index(GRID)
    sign = 1 - 2 * lax.axis_index("core")
    return jnp.clip((block - here) * sign + 1, 0, 2)


def encode_kernel(
    targets, x_hbm, weight_hbm, edges_hbm, across, own, mate, slope, laid, x, weight, edges, messages, arrived
):
    blocks, picks, rows, cols = edges.shape
    nodes = x.shape[0]
    chunks = 4
    step = nodes // chunks
    pieces = [slice(i * step, (i + 1) * step) for i in range(chunks)]
    copies = [pltpu.make_async_copy(weight_hbm, weight, arrived.at[0])]
    for i in range(chunks):
        copies.append(pltpu.make_async_copy(x_hbm.at[pieces[i]], x.at[pieces[i]], arrived.at[1 + i]))
    copies.append(pltpu.make_async_copy(edges_hbm, edges, arrived.at[1 + chunks]))
    for copy in copies:
        copy.start()
    laid[...] = jnp.zeros_like(laid)
    copies[0].wait()
    for i in range(chunks):
        copies[1 + i].wait()
        lifted, slanted = silu_and_slope(dot(x[pieces[i], :], weight[...], 1, 0))
        slope[pieces[i], :] = slanted.astype(BF)
        messages[pieces[i], :] = lifted.astype(BF)
    copies[1 + chunks].wait()
    for b in range(blocks):
        for k in range(picks):
            at = pl.ds(pl.multiple_of(slot_of(targets[k, b]) * rows, rows), rows)
            laid[at, b * cols : (b + 1) * cols] = edges[b, k]
    across[...] = dot(laid[:rows, :], messages[...], 1, 0).astype(BF)
    mate[...] = dot(laid[2 * rows :, :], messages[...], 1, 0).astype(BF)
    own[...] = dot(laid[rows : 2 * rows, :], messages[...], 1, 0).astype(BF)


def turn_kernel(laid, turned):
    turned[...] = laid[...].T


def sort_kernel(share, x, sorted_x):
    width = x.shape[1]
    row = lax.broadcasted_iota(jnp.int32, (width, width), 0)
    col = lax.broadcasted_iota(jnp.int32, (width, width), 1)
    half = width // 2
    ours = row // half
    inner = row % half
    core = lax.axis_index("core")
    side = jnp.where(ours == 1, core, 1 - core)
    wanted = (inner // share) * (2 * share) + side * share + inner % share
    pick = jnp.where(col == wanted, 1.0, 0.0).astype(BF)
    sorted_x[...] = dot(pick, x[...], 1, 1).astype(BF)


def update_kernel(across, own, mate, latent, weight, updated, again, slope):
    arrived = own[...].astype(F32) + across[...].astype(F32) + mate[...].astype(F32)
    lifted, slanted = silu_and_slope(dot(arrived.astype(BF), weight[...], 1, 0))
    slope[...] = slanted
    fresh = (latent[...].astype(F32) + lifted).astype(BF)
    updated[...] = fresh
    again[...] = fresh


def mix_kernel(sources, mixing, laid, turned):
    rows = mixing.shape[1]
    laid[...] = jnp.zeros_like(laid)
    for k in range(mixing.shape[0]):
        at = pl.ds(pl.multiple_of(slot_of(sources[0, k]) * rows, rows), rows)
        laid[:, at] = mixing[k]
    turned[...] = laid[...].T


def process_kernel(
    across, own, mate, mixing, turned, weight, cotangent, result, to_across, to_own, to_mate, near
):
    rows = own.shape[0]
    near[:rows, :] = across[...]
    near[rows : 2 * rows, :] = own[...]
    near[2 * rows :, :] = mate[...]
    processed = dot(mixing[...], near[...], 1, 0).astype(BF)
    lifted, slanted = silu_and_slope(dot(processed, weight[...], 1, 0))
    result[...] = (own[...].astype(F32) + lifted).astype(BF)
    delta = (cotangent[...].astype(F32) * slanted).astype(BF)
    back = dot(delta, weight[...], 1, 1).astype(BF)
    pushed = dot(turned[...], back, 1, 0).astype(BF)
    to_across[...], to_own[...], to_mate[...] = pushed[:rows], pushed[rows : 2 * rows], pushed[2 * rows :]


def return_kernel(across, own, mate, cotangent, slope, weight, grad, again):
    total = cotangent[...].astype(F32) + own[...].astype(F32)
    total = total + across[...].astype(F32) + mate[...].astype(F32)
    fresh = dot((total * slope[...]).astype(BF), weight[...], 1, 1).astype(BF)
    grad[...] = fresh
    again[...] = fresh


def message_kernel(across, own, mate, turned, slope, sorted_x, delta, theirs, near):
    rows = own.shape[0]
    near[:rows, :] = across[...]
    near[rows : 2 * rows, :] = own[...]
    near[2 * rows :, :] = mate[...]
    nodes = slope.shape[0]
    step = nodes // 4
    for i in range(4):
        at = slice(i * step, (i + 1) * step)
        grad = dot(turned[at, :], near[...], 1, 0)
        delta[at, :] = (grad * slope[at, :].astype(F32)).astype(BF)
    theirs[...] = dot(sorted_x[: theirs.shape[0], :], delta[...], 1, 0).astype(BF)


def gradient_kernel(sorted_x, delta, weight, ours, grid_grad):
    ours[...] = dot(sorted_x[ours.shape[0] :, :], delta[...], 1, 0)
    step = delta.shape[0] // 4
    for i in range(4):
        at = slice(i * step, (i + 1) * step)
        grid_grad[at, :] = dot(delta[at, :], weight[...], 1, 1).astype(BF)


def on_device(
    grid_latent, mesh_latent, cotangent, edge_weights, edge_targets,
    mesh_weights, mesh_sources, encode_weight, aggregate_weight, process_weight,
):
    members = lax.axis_size("ens")
    bands = lax.axis_size(GRID)
    mates, across_pairs = swap_pairs(bands)
    blocks, _, rows, _ = edge_weights.shape
    width = grid_latent.shape[2]
    half = width // 2

    def exchange(to_across, to_mate):
        from_mate = lax.ppermute(to_mate, GRID, mates)
        from_across = lax.ppermute(to_across, GRID, across_pairs)
        return from_across, from_mate

    nodes = blocks * rows
    grid_x = grid_latent[0]
    block = ((rows, width), BF)
    near = ((3 * rows, width), BF)
    to_across, own, to_mate, slope, laid = call(
        encode_kernel,
        [block, block, block, ((nodes, width), BF), ((3 * rows, nodes), BF)],
        [
            (grid_x.shape, BF), (encode_weight.shape, BF), (edge_weights.shape, BF),
            ((nodes, width), BF), pltpu.SemaphoreType.DMA((6,)),
        ],
        2 * nodes * width * (width + 3 * rows), 4 << 20,
        edge_targets.T, grid_x, encode_weight, edge_weights,
        copied=True,
    )
    across, mate = exchange(to_across, to_mate)
    sources, _ = lax.optimization_barrier((mesh_sources, slope))
    mixing, mixing_turned = call(
        mix_kernel, [((rows, 3 * rows), BF), ((3 * rows, rows), BF)], [], 0, 1 << 18,
        sources, mesh_weights[0],
    )
    updated, again, mesh_slope = call(
        update_kernel, [block, block, ((rows, width), F32)], [],
        2 * rows * width * width, 1 << 20,
        across, own, mate, mesh_latent[0], aggregate_weight,
    )
    across, mate = exchange(again, updated)
    later, grid_y, _ = lax.optimization_barrier((laid, grid_x, updated))
    turned = call(turn_kernel, [((nodes, 3 * rows), BF)], [], 0, 2 << 20, later)
    result, to_across, own, to_mate = call(
        process_kernel, [block] * 4, [near],
        4 * rows * width * width, 1 << 20,
        across, updated, mate, mixing, mixing_turned, process_weight, cotangent[0],
    )
    across, mate = exchange(to_across, to_mate)
    share = width // bands
    grid_y, _ = lax.optimization_barrier((grid_y, own))
    sorted_x = call(
        functools.partial(sort_kernel, share), [((width, nodes), BF)], [],
        2 * nodes * width * width, 2 << 20,
        grid_y,
    )
    agg_grad, again = call(
        return_kernel, [block, block], [],
        2 * rows * width * width, 1 << 20,
        across, own, mate, cotangent[0], mesh_slope, aggregate_weight,
    )
    across, mate = exchange(again, agg_grad)
    enc_delta, theirs = call(
        message_kernel, [((nodes, width), BF), ((half, width), BF)], [near],
        2 * nodes * width * (3 * rows + half), 4 << 20,
        across, agg_grad, mate, turned, slope, sorted_x,
    )
    arrived = lax.ppermute(theirs, GRID, mates)
    ours, grid_grad = call(
        gradient_kernel, [((half, width), F32), ((nodes, width), BF)], [],
        2 * nodes * width * (width + half), 4 << 20,
        sorted_x, enc_delta, encode_weight,
    )
    pair = (ours + arrived.astype(F32)).astype(BF)
    chips = bands // 2
    parts = lax.all_to_all(pair.reshape(chips, share, width), ("y", "z"), 0, 0)
    scale = 1.0 / float(members * nodes * bands) ** 0.5
    summed = parts.astype(F32).sum(0) * scale
    summed = jnp.broadcast_to(summed, (members, share, width))
    final = lax.all_to_all(summed, "ens", 0, 0).sum(0)
    return result[None], grid_grad[None], final


def solution(mesh):
    ens, bands = mesh.devices.shape
    fine = Mesh(mesh.devices.reshape((ens,) + grid_split(bands)), ("ens",) + GRID)
    return jax.shard_map(
        on_device,
        mesh=fine,
        in_specs=(
            P("ens", GRID, None),
            P("ens", GRID, None),
            P("ens", GRID, None),
            P(GRID, None, None, None),
            P(GRID, None),
            P(GRID, None, None, None),
            P(GRID, None),
            P(),
            P(),
            P(),
        ),
        out_specs=(P("ens", GRID, None), P("ens", GRID, None), P(GRID, None)),
        check_vma=False,
    )
```

time: 113 us -> 91.4 us (0.81)
  the two profiles are of different devices: /device:TPU:1 before, /device:TPU:2 now
where the time goes in v2:
time: 91.4 us; the launch traced here: 90.9 us
  blocking collectives  44.9 us (49%)
  starting transfers between devices  28.6 us (31%)
  Pallas kernels  11.4 us (12%)
  waiting for transfers between devices  2.14 us (2%)
  local copies, waits for them, and re-layouts  2.09 us (2%)
    all_to_all x1, blocking collectives, on_device(): parts = lax.all_to_all(pair.reshape(chips, share, width), ('y', 'z'), 0, 0)  36.3 us
    ppermute x4, starting transfers between devices, exchange(): from_mate = lax.ppermute(to_mate, GRID, mates)  23.7 us
    pallas_call x9, Pallas kernels, call(): pl.pallas_call(kernel, out_shape=shapes[0] if single else shapes, in_spec...  11.4 us
    all_to_all x1, blocking collectives, on_device(): final = lax.all_to_all(summed, 'ens', 0, 0).sum(0)  8.63 us
    ppermute x4, starting transfers between devices, exchange(): from_across = lax.ppermute(to_across, GRID, across_pairs)  2.93 us
    ppermute x4, waiting for transfers between devices, exchange(): from_mate = lax.ppermute(to_mate, GRID, mates)  2.12 us
    unnamed x22, local copies, waits for them, and re-layouts  2.02 us
    ppermute x1, starting transfers between devices, on_device(): arrived = lax.ppermute(theirs, GRID, mates)  1.92 us
  transfers between devices with their start and end apart: 9, of which 2 were waited for; matrix products, arithmetic and copies ran while one was open for 0% of the time, Pallas kernels for 4%

profile of v2, /device:TPU:2, one launch (start us, length us, event | category | flops | bytes accessed | tf_op | source)
XLA Modules:
  0.0 90.9 jit_solution(9684932490729549917)
XLA Ops:
  0.6 0.0 copy-start
  0.6 0.0 copy-start.6
  0.7 5.1 %shard_map.121 = (bf16[128,512]{1,0:T(8,128)(2,1)}, bf16[128,512]{1,0:T(8,128)(2,1)}, bf16[128,512]{1,0:T(8,128)(2,1)}, bf16[1024,512]{1,0:T(8,128)(2,1)}, bf16[384,1024]{1,0:T(8,128)(2,1)}) custom-call(s32[2,8]{1,0:T(2,128)} %bitcast.14, bf16[1024,512]{1,0:T(8,128)(2,1)} %bitcast.7, bf16[512,512]{1,0:T(8,128)(2,1)} %weight.7, bf16[8,2,128,128]{3,2,1,0:T(8,128)(2,1)} %edges_hbm.1), custom_call_target="tpu_custom_call" | custom-call | flops 939524096 | bytes 4194304 | tf_op jit(solution)/shard_map/pallas_call | solution.py:55
  5.8 0.7 collective-permute-start
  6.4 5.6 %collective-permute-start.1 = (bf16[128,512]{1,0:T(8,128)(2,1)}, bf16[128,512]{1,0:T(8,128)(2,1)S(1)}, u32[]{:S(2)}, u32[]{:S(2)}) collective-permute-start(bf16[128,512]{1,0:T(8,128)(2,1)} %get-tuple-element.29), channel_id=1, source_target_pairs={{0,1},{2,3},{4,5},{6,7},{8,9},{10,11},{12,13},{14,15},{16,17},{18,... | collective-permute-start | bytes 393224 | tf_op jit(solution)/shard_map/ppermute | solution.py:197
  12.1 0.0 collective-permute-done.across
  12.1 1.2 %collective-permute-done.1.mate = bf16[128,512]{1,0:T(8,128)(2,1)S(1)} collective-permute-done((bf16[128,512]{1,0:T(8,128)(2,1)}, bf16[128,512]{1,0:T(8,128)(2,1)S(1)}, u32[]{:S(2)}, u32[]{:S(2)}) %collective-permute-start.1) | collective-permute-done | bytes 131104 | tf_op jit(solution)/shard_map/ppermute | solution.py:197
  13.2 0.0 copy-done
  13.2 0.0 copy-done.6
  13.3 0.0 copy-start.7
  13.3 0.9 copy-done.7
  14.2 0.0 copy-start.8
  14.2 0.0 copy-start.4
  14.2 0.0 copy-start.5
  14.2 0.3 shard_map.122
  14.5 0.7 collective-permute-start.2
  15.1 5.6 %collective-permute-start.3 = (bf16[128,512]{1,0:T(8,128)(2,1)S(1)}, bf16[128,512]{1,0:T(8,128)(2,1)S(1)}, u32[]{:S(2)}, u32[]{:S(2)}) collective-permute-start(bf16[128,512]{1,0:T(8,128)(2,1)S(1)} %get-tuple-element.31.own), channel_id=1, source_target_pairs={{0,1},{2,3},{4,5},{6,7},{8,9},{10,11},{12,13},{14,15},{16,17},{18,... | collective-permute-start | bytes 393224 | tf_op jit(solution)/shard_map/ppermute | solution.py:197
  20.8 0.0 copy-start.9
  20.8 0.0 copy-done.8
  20.8 0.6 copy-done.9
  21.4 0.7 shard_map.123
  22.1 0.0 collective-permute-done.2.across
  22.1 0.0 collective-permute-done.3.mate
  22.1 0.0 copy-done.4
  22.1 0.0 copy-done.5
  22.1 1.1 %shard_map.124 = (bf16[128,512]{1,0:T(8,128)(2,1)}, bf16[128,512]{1,0:T(8,128)(2,1)S(1)}, bf16[128,512]{1,0:T(8,128)(2,1)S(1)}, bf16[128,512]{1,0:T(8,128)(2,1)S(1)}) custom-call(bf16[128,512]{1,0:T(8,128)(2,1)S(1)} %collective-permute-done.2.across, bf16[128,512]{1,0:T(8,128)(2,1)S(1)} %get-tuple-element.31.own, ...), custom_call_target="tpu_custom_call" | custom-call | flops 134217728 | bytes 1048576 | tf_op jit(solution)/shard_map/pallas_call | solution.py:55
  23.3 0.0 copy-start.3
  23.3 0.8 collective-permute-start.4
  24.1 5.6 %collective-permute-start.5 = (bf16[128,512]{1,0:T(8,128)(2,1)S(1)}, bf16[128,512]{1,0:T(8,128)(2,1)S(1)}, u32[]{:S(2)}, u32[]{:S(2)}) collective-permute-start(bf16[128,512]{1,0:T(8,128)(2,1)S(1)} %get-tuple-element.42), channel_id=1, source_target_pairs={{0,1},{2,3},{4,5},{6,7},{8,9},{10,11},{12,13},{14,15},{16,17},{18,... | collective-permute-start | bytes 393224 | tf_op jit(solution)/shard_map/ppermute | solution.py:197
  29.7 0.0 collective-permute-done.4.across
  29.7 1.0 %collective-permute-done.5.mate = bf16[128,512]{1,0:T(8,128)(2,1)S(1)} collective-permute-done((bf16[128,512]{1,0:T(8,128)(2,1)S(1)}, bf16[128,512]{1,0:T(8,128)(2,1)S(1)}, u32[]{:S(2)}, u32[]{:S(2)}) %collective-permute-start.5) | collective-permute-done | bytes 131104 | tf_op jit(solution)/shard_map/ppermute | solution.py:197
  30.7 0.3 shard_map.126
  31.0 0.0 copy-start.2
  31.0 0.8 collective-permute-start.6
  31.8 6.8 %collective-permute-start.7 = (bf16[128,512]{1,0:T(8,128)(2,1)S(1)}, bf16[128,512]{1,0:T(8,128)(2,1)S(1)}, u32[]{:S(2)}, u32[]{:S(2)}) collective-permute-start(bf16[128,512]{1,0:T(8,128)(2,1)S(1)} %get-tuple-element.45.own), channel_id=1, source_target_pairs={{0,1},{2,3},{4,5},{6,7},{8,9},{10,11},{12,13},{14,15},{16,17},{18,... | collective-permute-start | bytes 393224 | tf_op jit(solution)/shard_map/ppermute | solution.py:197
  38.7 0.0 copy-done.3
  38.7 0.3 shard_map.127.turned
  38.9 0.0 copy-done.2
  39.0 0.0 copy-start.1
  39.0 0.7 shard_map.125.sorted_x
  39.7 0.0 copy-start.10
  39.7 0.0 collective-permute-done.6.across
  39.7 0.0 collective-permute-done.7.mate
  39.8 0.4 copy-done.1
  40.2 1.0 %shard_map.128 = (bf16[1024,512]{1,0:T(8,128)(2,1)S(1)}, bf16[256,512]{1,0:T(8,128)(2,1)S(1)}) custom-call(bf16[128,512]{1,0:T(8,128)(2,1)S(1)} %collective-permute-done.6.across, bf16[128,512]{1,0:T(8,128)(2,1)S(1)} %get-tuple-element.45.own, bf16[128,512]{1,0:T(8,128)(2,1)S(1)} %collective-permute-done.7.mate, bf16[1024,384]{1,0:T(8,128)(2,1)S(1)} %shard_map.127.turned, ...), custom_call_target="tpu_custom_call" | custom-call | flops 671088640 | bytes 4194304 | tf_op jit(solution)/shard_map/pallas_call | solution.py:55
  41.2 1.9 %collective-permute-start.8 = (bf16[256,512]{1,0:T(8,128)(2,1)S(1)}, bf16[256,512]{1,0:T(8,128)(2,1)S(1)}, u32[]{:S(2)}, u32[]{:S(2)}) collective-permute-start(bf16[256,512]{1,0:T(8,128)(2,1)S(1)} %get-tuple-element.50), channel_id=1, source_target_pairs={{0,1},{2,3},{4,5},{6,7},{8,9},{10,11},{12,13},{14,15},{16,17},{18,... | collective-permute-start | bytes 786440 | tf_op jit(solution)/shard_map/ppermute | solution.py:254
  43.1 0.0 copy-done.10
  43.1 2.0 %shard_map.129 = (f32[256,512]{1,0:T(8,128)S(1)}, bf16[1024,512]{1,0:T(8,128)(2,1)}) custom-call(bf16[512,1024]{1,0:T(8,128)(2,1)S(1)} %shard_map.125.sorted_x, bf16[1024,512]{1,0:T(8,128)(2,1)S(1)} %get-tuple-element.47.delta, bf16[512,512]{1,0:T(8,128)(2,1)S(1)} %copy-done.10), custom_call_target="tpu_custom_call" | custom-call | flops 805306368 | bytes 4194304 | tf_op jit(solution)/shard_map/pallas_call | solution.py:55
  45.1 0.0 collective-permute-done.8
  45.1 0.1 add_convert_fusion
  45.1 0.1 reshape.9
  45.2 36.3 %all_to_all.10 = bf16[64,4,512]{2,1,0:T(4,128)(2,1)S(1)} all-to-all(bf16[64,4,512]{2,1,0:T(4,128)(2,1)S(1)} %reshape.9), channel_id=1, replica_groups=mesh['ens'=4,'y'=8,'z'=8,'core'=2] {'y','z'}, dimensions={0} | all-to-all | bytes 524288 | tf_op jit(solution)/shard_map/all_to_all | solution.py:262
  81.5 0.1 convert_reduce_fusion
  81.6 8.6 %all_to_all.11 = f32[4,4,512]{2,1,0:T(4,128)S(1)} all-to-all(f32[4,4,512]{2,1,0:T(4,128)S(1)} %broadcast_in_dim.11), channel_id=1, replica_groups=mesh['ens'=4,'y'=8,'z'=8,'core'=2] {'ens'}, dimensions={0} | all-to-all | bytes 65536 | tf_op jit(solution)/shard_map/all_to_all | solution.py:266
  90.3 0.6 reduce_sum.19
  (2 shorter events, 0.0 us)
Async XLA Ops:
  0.6 12.6 %copy-start = (bf16[512,512]{1,0:T(8,128)(2,1)S(1)}, bf16[512,512]{1,0:T(8,128)(2,1)}, u32[]{:S(2)}) copy-start(bf16[512,512]{1,0:T(8,128)(2,1)} %weight.6) | copy-start | bytes 1572868
  0.6 12.6 %copy-start.6 = (bf16[1,128,512]{2,1,0:T(8,128)(2,1)S(1)}, bf16[1,128,512]{2,1,0:T(8,128)(2,1)}, u32[]{:S(2)}) copy-start(bf16[1,128,512]{2,1,0:T(8,128)(2,1)} %param.11) | copy-start | bytes 393220
  5.8 6.3 %collective-permute-start = (bf16[128,512]{1,0:T(8,128)(2,1)}, bf16[128,512]{1,0:T(8,128)(2,1)S(1)}, u32[]{:S(2)}, u32[]{:S(2)}) collective-permute-start(bf16[128,512]{1,0:T(8,128)(2,1)} %get-tuple-element.27), channel_id=1, source_target_pairs={{1,2},{3,4},{5,6},{7,8},{9,10},{11,12},{13,14},{15,16},{17,18},{19... | collective-permute-start | bytes 393224 | tf_op jit(solution)/shard_map/ppermute | solution.py:198
  6.4 6.8 %collective-permute-start.1 = (bf16[128,512]{1,0:T(8,128)(2,1)}, bf16[128,512]{1,0:T(8,128)(2,1)S(1)}, u32[]{:S(2)}, u32[]{:S(2)}) collective-permute-start(bf16[128,512]{1,0:T(8,128)(2,1)} %get-tuple-element.29), channel_id=1, source_target_pairs={{0,1},{2,3},{4,5},{6,7},{8,9},{10,11},{12,13},{14,15},{16,17},{18,... | collective-permute-start | bytes 393224 | tf_op jit(solution)/shard_map/ppermute | solution.py:197
  13.3 0.9 copy-start.7
  14.2 6.6 %copy-start.8 = (bf16[1,2,128,128]{3,2,1,0:T(8,128)(2,1)S(1)}, bf16[1,2,128,128]{3,2,1,0:T(8,128)(2,1)}, u32[]{:S(2)}) copy-start(bf16[1,2,128,128]{3,2,1,0:T(8,128)(2,1)} %param.15) | copy-start | bytes 196612
  14.2 8.0 %copy-start.4 = (bf16[1,128,512]{2,1,0:T(8,128)(2,1)S(1)}, bf16[1,128,512]{2,1,0:T(8,128)(2,1)}, u32[]{:S(2)}) copy-start(bf16[1,128,512]{2,1,0:T(8,128)(2,1)} %param.12) | copy-start | bytes 393220
  14.2 8.0 %copy-start.5 = (bf16[512,512]{1,0:T(8,128)(2,1)S(1)}, bf16[512,512]{1,0:T(8,128)(2,1)}, u32[]{:S(2)}) copy-start(bf16[512,512]{1,0:T(8,128)(2,1)} %weight.5) | copy-start | bytes 1572868
  14.5 7.6 %collective-permute-start.2 = (bf16[128,512]{1,0:T(8,128)(2,1)S(1)}, bf16[128,512]{1,0:T(8,128)(2,1)S(1)}, u32[]{:S(2)}, u32[]{:S(2)}) collective-permute-start(bf16[128,512]{1,0:T(8,128)(2,1)S(1)} %get-tuple-element.30), channel_id=1, source_target_pairs={{1,2},{3,4},{5,6},{7,8},{9,10},{11,12},{13,14},{15,16},{17,18},{19... | collective-permute-start | bytes 393224 | tf_op jit(solution)/shard_map/ppermute | solution.py:198
  15.1 7.0 %collective-permute-start.3 = (bf16[128,512]{1,0:T(8,128)(2,1)S(1)}, bf16[128,512]{1,0:T(8,128)(2,1)S(1)}, u32[]{:S(2)}, u32[]{:S(2)}) collective-permute-start(bf16[128,512]{1,0:T(8,128)(2,1)S(1)} %get-tuple-element.31.own), channel_id=1, source_target_pairs={{0,1},{2,3},{4,5},{6,7},{8,9},{10,11},{12,13},{14,15},{16,17},{18,... | collective-permute-start | bytes 393224 | tf_op jit(solution)/shard_map/ppermute | solution.py:197
  20.8 0.7 copy-start.9
  23.3 15.4 %copy-start.3 = (bf16[384,1024]{1,0:T(8,128)(2,1)S(1)}, bf16[384,1024]{1,0:T(8,128)(2,1)}, u32[]{:S(2)}) copy-start(bf16[384,1024]{1,0:T(8,128)(2,1)} %get-tuple-element.46.laid) | copy-start | bytes 2359300
  23.3 6.4 %collective-permute-start.4 = (bf16[128,512]{1,0:T(8,128)(2,1)S(1)}, bf16[128,512]{1,0:T(8,128)(2,1)S(1)}, u32[]{:S(2)}, u32[]{:S(2)}) collective-permute-start(bf16[128,512]{1,0:T(8,128)(2,1)S(1)} %get-tuple-element.41), channel_id=1, source_target_pairs={{1,2},{3,4},{5,6},{7,8},{9,10},{11,12},{13,14},{15,16},{17,18},{19... | collective-permute-start | bytes 393224 | tf_op jit(solution)/shard_map/ppermute | solution.py:198
  24.1 6.6 %collective-permute-start.5 = (bf16[128,512]{1,0:T(8,128)(2,1)S(1)}, bf16[128,512]{1,0:T(8,128)(2,1)S(1)}, u32[]{:S(2)}, u32[]{:S(2)}) collective-permute-start(bf16[128,512]{1,0:T(8,128)(2,1)S(1)} %get-tuple-element.42), channel_id=1, source_target_pairs={{0,1},{2,3},{4,5},{6,7},{8,9},{10,11},{12,13},{14,15},{16,17},{18,... | collective-permute-start | bytes 393224 | tf_op jit(solution)/shard_map/ppermute | solution.py:197
  31.0 7.9 %copy-start.2 = (bf16[1,1024,512]{2,1,0:T(8,128)(2,1)S(1)}, bf16[1,1024,512]{2,1,0:T(8,128)(2,1)}, u32[]{:S(2)}) copy-start(bf16[1,1024,512]{2,1,0:T(8,128)(2,1)} %param.10) | copy-start | bytes 3145732
  31.0 8.7 %collective-permute-start.6 = (bf16[128,512]{1,0:T(8,128)(2,1)S(1)}, bf16[128,512]{1,0:T(8,128)(2,1)S(1)}, u32[]{:S(2)}, u32[]{:S(2)}) collective-permute-start(bf16[128,512]{1,0:T(8,128)(2,1)S(1)} %get-tuple-element.44), channel_id=1, source_target_pairs={{1,2},{3,4},{5,6},{7,8},{9,10},{11,12},{13,14},{15,16},{17,18},{19... | collective-permute-start | bytes 393224 | tf_op jit(solution)/shard_map/ppermute | solution.py:198
  31.8 7.9 %collective-permute-start.7 = (bf16[128,512]{1,0:T(8,128)(2,1)S(1)}, bf16[128,512]{1,0:T(8,128)(2,1)S(1)}, u32[]{:S(2)}, u32[]{:S(2)}) collective-permute-start(bf16[128,512]{1,0:T(8,128)(2,1)S(1)} %get-tuple-element.45.own), channel_id=1, source_target_pairs={{0,1},{2,3},{4,5},{6,7},{8,9},{10,11},{12,13},{14,15},{16,17},{18,... | collective-permute-start | bytes 393224 | tf_op jit(solution)/shard_map/ppermute | solution.py:197
  39.0 1.2 %copy-start.1 = (bf16[1024,512]{1,0:T(8,128)(2,1)S(1)}, bf16[1024,512]{1,0:T(8,128)(2,1)}, u32[]{:S(2)}) copy-start(bf16[1024,512]{1,0:T(8,128)(2,1)} %get-tuple-element.32.slope) | copy-start | bytes 3145732
  39.7 3.4 %copy-start.10 = (bf16[512,512]{1,0:T(8,128)(2,1)S(1)}, bf16[512,512]{1,0:T(8,128)(2,1)}, u32[]{:S(2)}) copy-start(bf16[512,512]{1,0:T(8,128)(2,1)} %weight.7) | copy-start | bytes 1572868
  41.2 3.9 %collective-permute-start.8 = (bf16[256,512]{1,0:T(8,128)(2,1)S(1)}, bf16[256,512]{1,0:T(8,128)(2,1)S(1)}, u32[]{:S(2)}, u32[]{:S(2)}) collective-permute-start(bf16[256,512]{1,0:T(8,128)(2,1)S(1)} %get-tuple-element.50), channel_id=1, source_target_pairs={{0,1},{2,3},{4,5},{6,7},{8,9},{10,11},{12,13},{14,15},{16,17},{18,... | collective-permute-start | bytes 786440 | tf_op jit(solution)/shard_map/ppermute | solution.py:254

commit v3 on v2

--- a/solution.py
+++ b/solution.py
@@ -10,6 +10,7 @@
 
 BF = jnp.bfloat16
 F32 = jnp.float32
+ENCODE_VMEM = 55992320
 GRID = ("y", "z", "core")
 
 
@@ -50,15 +51,15 @@
         for o in operands
     ]
     single = len(outs) == 1
-    shapes = [jax.ShapeDtypeStruct(shape, kind) for shape, kind in outs]
-    vmem = [pl.BlockSpec(memory_space=pltpu.VMEM) for _ in outs]
+    shapes = [jax.ShapeDtypeStruct(*o[:2]) for o in outs]
+    vmem = [pl.BlockSpec(memory_space=o[2] if len(o) > 2 else pltpu.VMEM) for o in outs]
     return pl.pallas_call(
         kernel,
         out_shape=shapes[0] if single else shapes,
         in_specs=specs,
         out_specs=vmem[0] if single else vmem,
         scratch_shapes=[pltpu.VMEM(*o) if isinstance(o, tuple) else o for o in scratch],
-        compiler_params=pltpu.CompilerParams(vmem_limit_bytes=(60 if copied else 24) << 20),
+        compiler_params=pltpu.CompilerParams(vmem_limit_bytes=ENCODE_VMEM if copied else 24 << 20),
         cost_estimate=pl.CostEstimate(flops=flops, bytes_accessed=moved, transcendentals=0),
     )(*operands)
 
@@ -70,34 +71,52 @@
 
 
 def encode_kernel(
-    targets, x_hbm, weight_hbm, edges_hbm, across, own, mate, slope, laid, x, weight, edges, messages, arrived
+    targets, x_hbm, weight_hbm, edges_hbm, across, own, mate, slope_hbm, laid_hbm,
+    x, weight, edges, messages, slope, laid, arrived, left,
 ):
     blocks, picks, rows, cols = edges.shape
     nodes = x.shape[0]
     chunks = 4
     step = nodes // chunks
     pieces = [slice(i * step, (i + 1) * step) for i in range(chunks)]
-    copies = [pltpu.make_async_copy(weight_hbm, weight, arrived.at[0])]
-    for i in range(chunks):
-        copies.append(pltpu.make_async_copy(x_hbm.at[pieces[i]], x.at[pieces[i]], arrived.at[1 + i]))
-    copies.append(pltpu.make_async_copy(edges_hbm, edges, arrived.at[1 + chunks]))
-    for copy in copies:
+    weight_in = pltpu.make_async_copy(weight_hbm, weight, arrived.at[0])
+    edges_in = pltpu.make_async_copy(edges_hbm, edges, arrived.at[1])
+    x_in = [
+        pltpu.make_async_copy(x_hbm.at[at], x.at[at], arrived.at[2 + i])
+        for i, at in enumerate(pieces)
+    ]
+    for copy in (weight_in, x_in[0], x_in[1], edges_in, x_in[2], x_in[3]):
         copy.start()
     laid[...] = jnp.zeros_like(laid)
-    copies[0].wait()
-    for i in range(chunks):
-        copies[1 + i].wait()
+
+    def encode(i):
         lifted, slanted = silu_and_slope(dot(x[pieces[i], :], weight[...], 1, 0))
         slope[pieces[i], :] = slanted.astype(BF)
         messages[pieces[i], :] = lifted.astype(BF)
-    copies[1 + chunks].wait()
+
+    weight_in.wait()
+    x_in[0].wait()
+    encode(0)
+    x_in[1].wait()
+    edges_in.wait()
     for b in range(blocks):
         for k in range(picks):
             at = pl.ds(pl.multiple_of(slot_of(targets[k, b]) * rows, rows), rows)
             laid[at, b * cols : (b + 1) * cols] = edges[b, k]
+    encode(1)
+    laid_out = pltpu.make_async_copy(laid, laid_hbm, left.at[0])
+    laid_out.start()
+    x_in[2].wait()
+    x_in[3].wait()
+    encode(2)
+    encode(3)
+    slope_out = pltpu.make_async_copy(slope, slope_hbm, left.at[1])
+    slope_out.start()
     across[...] = dot(laid[:rows, :], messages[...], 1, 0).astype(BF)
+    own[...] = dot(laid[rows : 2 * rows, :], messages[...], 1, 0).astype(BF)
     mate[...] = dot(laid[2 * rows :, :], messages[...], 1, 0).astype(BF)
-    own[...] = dot(laid[rows : 2 * rows, :], messages[...], 1, 0).astype(BF)
+    laid_out.wait()
+    slope_out.wait()
 
 
 def turn_kernel(laid, turned):
@@ -204,10 +223,11 @@
     near = ((3 * rows, width), BF)
     to_across, own, to_mate, slope, laid = call(
         encode_kernel,
-        [block, block, block, ((nodes, width), BF), ((3 * rows, nodes), BF)],
+        [block, block, block, ((nodes, width), BF, pltpu.HBM), ((3 * rows, nodes), BF, pltpu.HBM)],
         [
             (grid_x.shape, BF), (encode_weight.shape, BF), (edge_weights.shape, BF),
-            ((nodes, width), BF), pltpu.SemaphoreType.DMA((6,)),
+            ((nodes, width), BF), ((nodes, width), BF), ((3 * rows, nodes), BF),
+            pltpu.SemaphoreType.DMA((6,)), pltpu.SemaphoreType.DMA((2,)),
         ],
         2 * nodes * width * (width + 3 * rows), 4 << 20,
         edge_targets.T, grid_x, encode_weight, edge_weights,
@@ -219,6 +239,7 @@
         mix_kernel, [((rows, 3 * rows), BF), ((3 * rows, rows), BF)], [], 0, 1 << 18,
         sources, mesh_weights[0],
     )
+    own, mixing = lax.optimization_barrier((own, mixing))
     updated, again, mesh_slope = call(
         update_kernel, [block, block, ((rows, width), F32)], [],
         2 * rows * width * width, 1 << 20,
@@ -240,6 +261,7 @@
         2 * nodes * width * width, 2 << 20,
         grid_y,
     )
+    own, sorted_x = lax.optimization_barrier((own, sorted_x))
     agg_grad, again = call(
         return_kernel, [block, block], [],
         2 * rows * width * width, 1 << 20,

time: 91.4 us -> 90.2 us (0.987)
  transfers between devices with their start and end apart: 9 -> 9, of which waited for: 2 -> 3; matrix products, arithmetic and copies ran while one was open for 0% -> 0% of each run, Pallas kernels for 4% -> 4%
where the time goes in v3:
time: 90.2 us; the launch traced here: 89.8 us
  blocking collectives  45.1 us (50%)
  starting transfers between devices  28.8 us (32%)
  Pallas kernels  10.9 us (12%)
  waiting for transfers between devices  1.82 us (2%)
  local copies, waits for them, and re-layouts  1.43 us (2%)
  between operations  0.91 us (1%)
    all_to_all x1, blocking collectives, on_device(): parts = lax.all_to_all(pair.reshape(chips, share, width), ('y', 'z'), 0, 0)  36.5 us
    ppermute x4, starting transfers between devices, exchange(): from_mate = lax.ppermute(to_mate, GRID, mates)  23.8 us
    pallas_call x9, Pallas kernels, call(): pl.pallas_call(kernel, out_shape=shapes[0] if single else shapes, in_spec...  10.9 us
    all_to_all x1, blocking collectives, on_device(): final = lax.all_to_all(summed, 'ens', 0, 0).sum(0)  8.62 us
    ppermute x4, starting transfers between devices, exchange(): from_across = lax.ppermute(to_across, GRID, across_pairs)  2.8 us
    ppermute x1, starting transfers between devices, on_device(): arrived = lax.ppermute(theirs, GRID, mates)  2.27 us
    ppermute x4, waiting for transfers between devices, exchange(): from_mate = lax.ppermute(to_mate, GRID, mates)  1.81 us
  transfers between devices with their start and end apart: 9, of which 3 were waited for; matrix products, arithmetic and copies ran while one was open for 0% of the time, Pallas kernels for 4%

profile of v3, /device:TPU:2, one launch (start us, length us, event | category | flops | bytes accessed | tf_op | source)
XLA Modules:
  0.0 89.8 jit_solution(10446773885321506779)
XLA Ops:
  0.6 0.0 copy-start.10
  0.6 0.7 copy-done.10
  1.3 0.0 copy-start.7
  1.3 0.0 copy-start
  1.3 0.0 copy-start.6
  1.3 4.6 %shard_map.121 = (bf16[128,512]{1,0:T(8,128)(2,1)S(1)}, bf16[128,512]{1,0:T(8,128)(2,1)S(1)}, bf16[128,512]{1,0:T(8,128)(2,1)S(1)}, bf16[1024,512]{1,0:T(8,128)(2,1)}, bf16[384,1024]{1,0:T(8,128)(2,1)}) custom-call(s32[2,8]{1,0:T(2,128)S(1)} %bitcast.13, bf16[1024,512]{1,0:T(8,128)(2,1)} %bitcast.7, bf16[512,512]{1,0:T(8,128)(2,1)} %weight.7, ...), custom_call_target="tpu_custom_call" | custom-call | flops 939524096 | bytes 4194304 | tf_op jit(solution)/shard_map/pallas_call | solution.py:56
  5.9 0.7 collective-permute-start
  6.6 5.6 %collective-permute-start.1 = (bf16[128,512]{1,0:T(8,128)(2,1)S(1)}, bf16[128,512]{1,0:T(8,128)(2,1)S(1)}, u32[]{:S(2)}, u32[]{:S(2)}) collective-permute-start(bf16[128,512]{1,0:T(8,128)(2,1)S(1)} %get-tuple-element.37), channel_id=1, source_target_pairs={{0,1},{2,3},{4,5},{6,7},{8,9},{10,11},{12,13},{14,15},{16,17},{18,... | collective-permute-start | bytes 393224 | tf_op jit(solution)/shard_map/ppermute | solution.py:216
  12.2 0.0 copy-start.8
  12.2 0.0 copy-done.7
  12.2 0.6 copy-done.8
  12.9 0.0 copy-start.4
  12.9 0.0 copy-start.5
  12.9 0.7 shard_map.122
  13.5 0.0 collective-permute-done.across
  13.5 0.0 collective-permute-done.1.mate
  13.5 0.0 copy-done
  13.6 0.0 copy-done.6
  13.6 0.0 copy-start.2
  13.6 0.3 shard_map.123
  13.9 0.7 collective-permute-start.2
  14.6 5.6 %collective-permute-start.3 = (bf16[128,512]{1,0:T(8,128)(2,1)S(1)}, bf16[128,512]{1,0:T(8,128)(2,1)S(1)}, u32[]{:S(2)}, u32[]{:S(2)}) collective-permute-start(bf16[128,512]{1,0:T(8,128)(2,1)S(1)} %get-tuple-element.39.own), channel_id=1, source_target_pairs={{0,1},{2,3},{4,5},{6,7},{8,9},{10,11},{12,13},{14,15},{16,17},{18,... | collective-permute-start | bytes 393224 | tf_op jit(solution)/shard_map/ppermute | solution.py:216
  20.2 0.0 collective-permute-done.2.across
  20.2 1.0 %collective-permute-done.3.mate = bf16[128,512]{1,0:T(8,128)(2,1)S(1)} collective-permute-done((bf16[128,512]{1,0:T(8,128)(2,1)S(1)}, bf16[128,512]{1,0:T(8,128)(2,1)S(1)}, u32[]{:S(2)}, u32[]{:S(2)}) %collective-permute-start.3) | collective-permute-done | bytes 131104 | tf_op jit(solution)/shard_map/ppermute | solution.py:216
  21.2 0.0 copy-done.4
  21.2 0.0 copy-done.5
  21.2 1.1 %shard_map.124 = (bf16[128,512]{1,0:T(8,128)(2,1)}, bf16[128,512]{1,0:T(8,128)(2,1)S(1)}, bf16[128,512]{1,0:T(8,128)(2,1)S(1)}, bf16[128,512]{1,0:T(8,128)(2,1)S(1)}) custom-call(bf16[128,512]{1,0:T(8,128)(2,1)S(1)} %collective-permute-done.2.across, bf16[128,512]{1,0:T(8,128)(2,1)S(1)} %get-tuple-element.39.own, ...), custom_call_target="tpu_custom_call" | custom-call | flops 134217728 | bytes 1048576 | tf_op jit(solution)/shard_map/pallas_call | solution.py:56
  22.3 0.7 collective-permute-start.4
  23.0 5.6 %collective-permute-start.5 = (bf16[128,512]{1,0:T(8,128)(2,1)S(1)}, bf16[128,512]{1,0:T(8,128)(2,1)S(1)}, u32[]{:S(2)}, u32[]{:S(2)}) collective-permute-start(bf16[128,512]{1,0:T(8,128)(2,1)S(1)} %get-tuple-element.50), channel_id=1, source_target_pairs={{0,1},{2,3},{4,5},{6,7},{8,9},{10,11},{12,13},{14,15},{16,17},{18,... | collective-permute-start | bytes 393224 | tf_op jit(solution)/shard_map/ppermute | solution.py:216
  28.6 0.0 copy-done.2
  28.6 0.7 shard_map.125.sorted_x
  29.4 0.0 copy-start.3
  29.4 0.0 collective-permute-done.4.across
  29.4 0.2 collective-permute-done.5.mate
  29.6 0.3 shard_map.126
  29.9 0.0 copy-start.1
  29.9 0.8 collective-permute-start.6
  30.7 6.8 %collective-permute-start.7 = (bf16[128,512]{1,0:T(8,128)(2,1)S(1)}, bf16[128,512]{1,0:T(8,128)(2,1)S(1)}, u32[]{:S(2)}, u32[]{:S(2)}) collective-permute-start(bf16[128,512]{1,0:T(8,128)(2,1)S(1)} %get-tuple-element.53.own), channel_id=1, source_target_pairs={{0,1},{2,3},{4,5},{6,7},{8,9},{10,11},{12,13},{14,15},{16,17},{18,... | collective-permute-start | bytes 393224 | tf_op jit(solution)/shard_map/ppermute | solution.py:216
  37.6 0.0 copy-done.3
  37.6 0.3 shard_map.127.turned
  37.8 0.0 copy-start.9
  37.9 0.0 collective-permute-done.6.across
  37.9 0.7 collective-permute-done.7.mate
  38.5 0.0 copy-done.1
  38.5 1.0 %shard_map.128 = (bf16[1024,512]{1,0:T(8,128)(2,1)S(1)}, bf16[256,512]{1,0:T(8,128)(2,1)S(1)}) custom-call(bf16[128,512]{1,0:T(8,128)(2,1)S(1)} %collective-permute-done.6.across, bf16[128,512]{1,0:T(8,128)(2,1)S(1)} %get-tuple-element.53.own, bf16[128,512]{1,0:T(8,128)(2,1)S(1)} %collective-permute-done.7.mate, bf16[1024,384]{1,0:T(8,128)(2,1)S(1)} %shard_map.127.turned, ...), custom_call_target="tpu_custom_call" | custom-call | flops 671088640 | bytes 4194304 | tf_op jit(solution)/shard_map/pallas_call | solution.py:56
  39.5 2.3 %collective-permute-start.8 = (bf16[256,512]{1,0:T(8,128)(2,1)S(1)}, bf16[256,512]{1,0:T(8,128)(2,1)S(1)}, u32[]{:S(2)}, u32[]{:S(2)}) collective-permute-start(bf16[256,512]{1,0:T(8,128)(2,1)S(1)} %get-tuple-element.58), channel_id=1, source_target_pairs={{0,1},{2,3},{4,5},{6,7},{8,9},{10,11},{12,13},{14,15},{16,17},{18,... | collective-permute-start | bytes 786440 | tf_op jit(solution)/shard_map/ppermute | solution.py:276
  41.8 0.0 copy-done.9
  41.8 2.0 %shard_map.129 = (f32[256,512]{1,0:T(8,128)S(1)}, bf16[1024,512]{1,0:T(8,128)(2,1)}) custom-call(bf16[512,1024]{1,0:T(8,128)(2,1)S(1)} %shard_map.125.sorted_x, bf16[1024,512]{1,0:T(8,128)(2,1)S(1)} %get-tuple-element.55.delta, bf16[512,512]{1,0:T(8,128)(2,1)S(1)} %copy-done.9), custom_call_target="tpu_custom_call" | custom-call | flops 805306368 | bytes 4194304 | tf_op jit(solution)/shard_map/pallas_call | solution.py:56
  43.8 0.0 collective-permute-done.8
  43.8 0.1 add_convert_fusion
  43.8 0.1 reshape.9
  43.9 36.5 %all_to_all.10 = bf16[64,4,512]{2,1,0:T(4,128)(2,1)S(1)} all-to-all(bf16[64,4,512]{2,1,0:T(4,128)(2,1)S(1)} %reshape.9), channel_id=1, replica_groups=mesh['ens'=4,'y'=8,'z'=8,'core'=2] {'y','z'}, dimensions={0} | all-to-all | bytes 524288 | tf_op jit(solution)/shard_map/all_to_all | solution.py:284
  80.4 0.1 convert_reduce_fusion
  80.5 8.6 %all_to_all.11 = f32[4,4,512]{2,1,0:T(4,128)S(1)} all-to-all(f32[4,4,512]{2,1,0:T(4,128)S(1)} %broadcast_in_dim.11), channel_id=1, replica_groups=mesh['ens'=4,'y'=8,'z'=8,'core'=2] {'ens'}, dimensions={0} | all-to-all | bytes 65536 | tf_op jit(solution)/shard_map/all_to_all | solution.py:288
  89.2 0.6 reduce_sum.19
  (2 shorter events, 0.0 us)
Async XLA Ops:
  0.6 0.7 copy-start.10
  1.3 10.9 %copy-start.7 = (bf16[1,2,128,128]{3,2,1,0:T(8,128)(2,1)S(1)}, bf16[1,2,128,128]{3,2,1,0:T(8,128)(2,1)}, u32[]{:S(2)}) copy-start(bf16[1,2,128,128]{3,2,1,0:T(8,128)(2,1)} %param.15) | copy-start | bytes 196612
  1.3 12.2 %copy-start = (bf16[512,512]{1,0:T(8,128)(2,1)S(1)}, bf16[512,512]{1,0:T(8,128)(2,1)}, u32[]{:S(2)}) copy-start(bf16[512,512]{1,0:T(8,128)(2,1)} %weight.6) | copy-start | bytes 1572868
  1.3 12.2 %copy-start.6 = (bf16[1,128,512]{2,1,0:T(8,128)(2,1)S(1)}, bf16[1,128,512]{2,1,0:T(8,128)(2,1)}, u32[]{:S(2)}) copy-start(bf16[1,128,512]{2,1,0:T(8,128)(2,1)} %param.11) | copy-start | bytes 393220
  5.9 7.6 %collective-permute-start = (bf16[128,512]{1,0:T(8,128)(2,1)S(1)}, bf16[128,512]{1,0:T(8,128)(2,1)S(1)}, u32[]{:S(2)}, u32[]{:S(2)}) collective-permute-start(bf16[128,512]{1,0:T(8,128)(2,1)S(1)} %get-tuple-element.31), channel_id=1, source_target_pairs={{1,2},{3,4},{5,6},{7,8},{9,10},{11,12},{13,14},{15,16},{17,18},{19... | collective-permute-start | bytes 393224 | tf_op jit(solution)/shard_map/ppermute | solution.py:217
  6.6 7.0 %collective-permute-start.1 = (bf16[128,512]{1,0:T(8,128)(2,1)S(1)}, bf16[128,512]{1,0:T(8,128)(2,1)S(1)}, u32[]{:S(2)}, u32[]{:S(2)}) collective-permute-start(bf16[128,512]{1,0:T(8,128)(2,1)S(1)} %get-tuple-element.37), channel_id=1, source_target_pairs={{0,1},{2,3},{4,5},{6,7},{8,9},{10,11},{12,13},{14,15},{16,17},{18,... | collective-permute-start | bytes 393224 | tf_op jit(solution)/shard_map/ppermute | solution.py:216
  12.2 0.7 copy-start.8
  12.9 8.3 %copy-start.4 = (bf16[1,128,512]{2,1,0:T(8,128)(2,1)S(1)}, bf16[1,128,512]{2,1,0:T(8,128)(2,1)}, u32[]{:S(2)}) copy-start(bf16[1,128,512]{2,1,0:T(8,128)(2,1)} %param.12) | copy-start | bytes 393220
  12.9 8.3 %copy-start.5 = (bf16[512,512]{1,0:T(8,128)(2,1)S(1)}, bf16[512,512]{1,0:T(8,128)(2,1)}, u32[]{:S(2)}) copy-start(bf16[512,512]{1,0:T(8,128)(2,1)} %weight.5) | copy-start | bytes 1572868
  13.6 15.1 %copy-start.2 = (bf16[1,1024,512]{2,1,0:T(8,128)(2,1)S(1)}, bf16[1,1024,512]{2,1,0:T(8,128)(2,1)}, u32[]{:S(2)}) copy-start(bf16[1,1024,512]{2,1,0:T(8,128)(2,1)} %param.10) | copy-start | bytes 3145732
  13.9 6.3 %collective-permute-start.2 = (bf16[128,512]{1,0:T(8,128)(2,1)S(1)}, bf16[128,512]{1,0:T(8,128)(2,1)S(1)}, u32[]{:S(2)}, u32[]{:S(2)}) collective-permute-start(bf16[128,512]{1,0:T(8,128)(2,1)S(1)} %get-tuple-element.38), channel_id=1, source_target_pairs={{1,2},{3,4},{5,6},{7,8},{9,10},{11,12},{13,14},{15,16},{17,18},{19... | collective-permute-start | bytes 393224 | tf_op jit(solution)/shard_map/ppermute | solution.py:217
  14.6 6.6 %collective-permute-start.3 = (bf16[128,512]{1,0:T(8,128)(2,1)S(1)}, bf16[128,512]{1,0:T(8,128)(2,1)S(1)}, u32[]{:S(2)}, u32[]{:S(2)}) collective-permute-start(bf16[128,512]{1,0:T(8,128)(2,1)S(1)} %get-tuple-element.39.own), channel_id=1, source_target_pairs={{0,1},{2,3},{4,5},{6,7},{8,9},{10,11},{12,13},{14,15},{16,17},{18,... | collective-permute-start | bytes 393224 | tf_op jit(solution)/shard_map/ppermute | solution.py:216
  22.3 7.1 %collective-permute-start.4 = (bf16[128,512]{1,0:T(8,128)(2,1)S(1)}, bf16[128,512]{1,0:T(8,128)(2,1)S(1)}, u32[]{:S(2)}, u32[]{:S(2)}) collective-permute-start(bf16[128,512]{1,0:T(8,128)(2,1)S(1)} %get-tuple-element.48), channel_id=1, source_target_pairs={{1,2},{3,4},{5,6},{7,8},{9,10},{11,12},{13,14},{15,16},{17,18},{19... | collective-permute-start | bytes 393224 | tf_op jit(solution)/shard_map/ppermute | solution.py:217
  23.0 6.6 %collective-permute-start.5 = (bf16[128,512]{1,0:T(8,128)(2,1)S(1)}, bf16[128,512]{1,0:T(8,128)(2,1)S(1)}, u32[]{:S(2)}, u32[]{:S(2)}) collective-permute-start(bf16[128,512]{1,0:T(8,128)(2,1)S(1)} %get-tuple-element.50), channel_id=1, source_target_pairs={{0,1},{2,3},{4,5},{6,7},{8,9},{10,11},{12,13},{14,15},{16,17},{18,... | collective-permute-start | bytes 393224 | tf_op jit(solution)/shard_map/ppermute | solution.py:216
  29.4 8.2 %copy-start.3 = (bf16[384,1024]{1,0:T(8,128)(2,1)S(1)}, bf16[384,1024]{1,0:T(8,128)(2,1)}, u32[]{:S(2)}) copy-start(bf16[384,1024]{1,0:T(8,128)(2,1)} %get-tuple-element.54.laid) | copy-start | bytes 2359300
  29.9 8.6 %copy-start.1 = (bf16[1024,512]{1,0:T(8,128)(2,1)S(1)}, bf16[1024,512]{1,0:T(8,128)(2,1)}, u32[]{:S(2)}) copy-start(bf16[1024,512]{1,0:T(8,128)(2,1)} %get-tuple-element.33.slope) | copy-start | bytes 3145732
  29.9 7.9 %collective-permute-start.6 = (bf16[128,512]{1,0:T(8,128)(2,1)S(1)}, bf16[128,512]{1,0:T(8,128)(2,1)S(1)}, u32[]{:S(2)}, u32[]{:S(2)}) collective-permute-start(bf16[128,512]{1,0:T(8,128)(2,1)S(1)} %get-tuple-element.52), channel_id=1, source_target_pairs={{1,2},{3,4},{5,6},{7,8},{9,10},{11,12},{13,14},{15,16},{17,18},{19... | collective-permute-start | bytes 393224 | tf_op jit(solution)/shard_map/ppermute | solution.py:217
  30.7 7.8 %collective-permute-start.7 = (bf16[128,512]{1,0:T(8,128)(2,1)S(1)}, bf16[128,512]{1,0:T(8,128)(2,1)S(1)}, u32[]{:S(2)}, u32[]{:S(2)}) collective-permute-start(bf16[128,512]{1,0:T(8,128)(2,1)S(1)} %get-tuple-element.53.own), channel_id=1, source_target_pairs={{0,1},{2,3},{4,5},{6,7},{8,9},{10,11},{12,13},{14,15},{16,17},{18,... | collective-permute-start | bytes 393224 | tf_op jit(solution)/shard_map/ppermute | solution.py:216
  37.8 4.0 %copy-start.9 = (bf16[512,512]{1,0:T(8,128)(2,1)S(1)}, bf16[512,512]{1,0:T(8,128)(2,1)}, u32[]{:S(2)}) copy-start(bf16[512,512]{1,0:T(8,128)(2,1)} %weight.7) | copy-start | bytes 1572868
  39.5 4.2 %collective-permute-start.8 = (bf16[256,512]{1,0:T(8,128)(2,1)S(1)}, bf16[256,512]{1,0:T(8,128)(2,1)S(1)}, u32[]{:S(2)}, u32[]{:S(2)}) collective-permute-start(bf16[256,512]{1,0:T(8,128)(2,1)S(1)} %get-tuple-element.58), channel_id=1, source_target_pairs={{0,1},{2,3},{4,5},{6,7},{8,9},{10,11},{12,13},{14,15},{16,17},{18,... | collective-permute-start | bytes 786440 | tf_op jit(solution)/shard_map/ppermute | solution.py:276

commit v4 on v3

--- a/solution.py
+++ b/solution.py
@@ -71,8 +71,8 @@
 
 
 def encode_kernel(
-    targets, x_hbm, weight_hbm, edges_hbm, across, own, mate, slope_hbm, laid_hbm,
-    x, weight, edges, messages, slope, laid, arrived, left,
+    targets, x_hbm, weight_hbm, edges_hbm, across, own, mate, laid_hbm,
+    x, weight, edges, messages, laid, arrived, left,
 ):
     blocks, picks, rows, cols = edges.shape
     nodes = x.shape[0]
@@ -90,9 +90,8 @@
     laid[...] = jnp.zeros_like(laid)
 
     def encode(i):
-        lifted, slanted = silu_and_slope(dot(x[pieces[i], :], weight[...], 1, 0))
-        slope[pieces[i], :] = slanted.astype(BF)
-        messages[pieces[i], :] = lifted.astype(BF)
+        encoded = dot(x[pieces[i], :], weight[...], 1, 0)
+        messages[pieces[i], :] = (encoded * sigmoid(encoded)).astype(BF)
 
     weight_in.wait()
     x_in[0].wait()
@@ -104,23 +103,28 @@
             at = pl.ds(pl.multiple_of(slot_of(targets[k, b]) * rows, rows), rows)
             laid[at, b * cols : (b + 1) * cols] = edges[b, k]
     encode(1)
-    laid_out = pltpu.make_async_copy(laid, laid_hbm, left.at[0])
+    laid_out = pltpu.make_async_copy(laid, laid_hbm, left)
     laid_out.start()
     x_in[2].wait()
     x_in[3].wait()
     encode(2)
     encode(3)
-    slope_out = pltpu.make_async_copy(slope, slope_hbm, left.at[1])
-    slope_out.start()
     across[...] = dot(laid[:rows, :], messages[...], 1, 0).astype(BF)
     own[...] = dot(laid[rows : 2 * rows, :], messages[...], 1, 0).astype(BF)
     mate[...] = dot(laid[2 * rows :, :], messages[...], 1, 0).astype(BF)
     laid_out.wait()
-    slope_out.wait()
-
-
-def turn_kernel(laid, turned):
+
+
+def slope_kernel(x, weight, slope):
+    step = x.shape[0] // 4
+    for i in range(4):
+        at = slice(i * step, (i + 1) * step)
+        slope[at, :] = silu_and_slope(dot(x[at, :], weight[...], 1, 0))[1].astype(BF)
+
+
+def turn_kernel(laid, weight, turned, weight_turned):
     turned[...] = laid[...].T
+    weight_turned[...] = weight[...].T
 
 
 def sort_kernel(share, x, sorted_x):
@@ -193,12 +197,18 @@
     theirs[...] = dot(sorted_x[: theirs.shape[0], :], delta[...], 1, 0).astype(BF)
 
 
-def gradient_kernel(sorted_x, delta, weight, ours, grid_grad):
+def gradient_kernel(sorted_x, delta, weight_turned, ours, grid_grad_hbm, grid_grad, left):
+    chunks = 4
+    step = delta.shape[0] // chunks
+    copies = []
+    for i in range(chunks):
+        at = slice(i * step, (i + 1) * step)
+        grid_grad[at, :] = dot(delta[at, :], weight_turned[...], 1, 0).astype(BF)
+        copies.append(pltpu.make_async_copy(grid_grad.at[at], grid_grad_hbm.at[at], left.at[i]))
+        copies[i].start()
     ours[...] = dot(sorted_x[ours.shape[0] :, :], delta[...], 1, 0)
-    step = delta.shape[0] // 4
-    for i in range(4):
-        at = slice(i * step, (i + 1) * step)
-        grid_grad[at, :] = dot(delta[at, :], weight[...], 1, 1).astype(BF)
+    for copy in copies:
+        copy.wait()
 
 
 def on_device(
@@ -221,20 +231,20 @@
     grid_x = grid_latent[0]
     block = ((rows, width), BF)
     near = ((3 * rows, width), BF)
-    to_across, own, to_mate, slope, laid = call(
+    to_across, own, to_mate, laid = call(
         encode_kernel,
-        [block, block, block, ((nodes, width), BF, pltpu.HBM), ((3 * rows, nodes), BF, pltpu.HBM)],
+        [block, block, block, ((3 * rows, nodes), BF, pltpu.HBM)],
         [
             (grid_x.shape, BF), (encode_weight.shape, BF), (edge_weights.shape, BF),
-            ((nodes, width), BF), ((nodes, width), BF), ((3 * rows, nodes), BF),
-            pltpu.SemaphoreType.DMA((6,)), pltpu.SemaphoreType.DMA((2,)),
+            ((nodes, width), BF), ((3 * rows, nodes), BF),
+            pltpu.SemaphoreType.DMA((6,)), pltpu.SemaphoreType.DMA,
         ],
         2 * nodes * width * (width + 3 * rows), 4 << 20,
         edge_targets.T, grid_x, encode_weight, edge_weights,
         copied=True,
     )
     across, mate = exchange(to_across, to_mate)
-    sources, _ = lax.optimization_barrier((mesh_sources, slope))
+    sources, _ = lax.optimization_barrier((mesh_sources, laid))
     mixing, mixing_turned = call(
         mix_kernel, [((rows, 3 * rows), BF), ((3 * rows, rows), BF)], [], 0, 1 << 18,
         sources, mesh_weights[0],
@@ -246,8 +256,16 @@
         across, own, mate, mesh_latent[0], aggregate_weight,
     )
     across, mate = exchange(again, updated)
-    later, grid_y, _ = lax.optimization_barrier((laid, grid_x, updated))
-    turned = call(turn_kernel, [((nodes, 3 * rows), BF)], [], 0, 2 << 20, later)
+    later, grid_y, weight, _ = lax.optimization_barrier((laid, grid_x, encode_weight, updated))
+    slope = call(
+        slope_kernel, [((nodes, width), BF)], [],
+        2 * nodes * width * width, 3 << 20,
+        grid_y, weight,
+    )
+    turned, weight_turned = call(
+        turn_kernel, [((nodes, 3 * rows), BF), ((width, width), BF)], [], 0, 2 << 20, later, weight
+    )
+    updated, slope = lax.optimization_barrier((updated, slope))
     result, to_across, own, to_mate = call(
         process_kernel, [block] * 4, [near],
         4 * rows * width * width, 1 << 20,
@@ -275,9 +293,11 @@
     )
     arrived = lax.ppermute(theirs, GRID, mates)
     ours, grid_grad = call(
-        gradient_kernel, [((half, width), F32), ((nodes, width), BF)], [],
+        gradient_kernel,
+        [((half, width), F32), ((nodes, width), BF, pltpu.HBM)],
+        [((nodes, width), BF), pltpu.SemaphoreType.DMA((4,))],
         2 * nodes * width * (width + half), 4 << 20,
-        sorted_x, enc_delta, encode_weight,
+        sorted_x, enc_delta, weight_turned,
     )
     pair = (ours + arrived.astype(F32)).astype(BF)
     chips = bands // 2

time: 90.2 us -> 88.7 us (0.983)
    pallas_call x9 -> x10, Pallas kernels: 10.9 us -> 10.3 us  [call(): pl.pallas_call(kernel, out_shape=shapes[0] if single else shapes, in_spec...]
  transfers between devices with their start and end apart: 9 -> 9, of which waited for: 3 -> 3; matrix products, arithmetic and copies ran while one was open for 0% -> 0% of each run, Pallas kernels for 4% -> 5%
where the time goes in v4:
time: 88.7 us; the launch traced here: 88.2 us
  blocking collectives  45.3 us (51%)
  starting transfers between devices  29 us (33%)
  Pallas kernels  10.3 us (12%)
  waiting for transfers between devices  1.03 us (1%)
  between operations  0.94 us (1%)
    all_to_all x1, blocking collectives, on_device(): parts = lax.all_to_all(pair.reshape(chips, share, width), ('y', 'z'), 0, 0)  36.7 us
    ppermute x4, starting transfers between devices, exchange(): from_mate = lax.ppermute(to_mate, GRID, mates)  23.9 us
    pallas_call x10, Pallas kernels, call(): pl.pallas_call(kernel, out_shape=shapes[0] if single else shapes, in_spec...  10.3 us
    all_to_all x1, blocking collectives, on_device(): final = lax.all_to_all(summed, 'ens', 0, 0).sum(0)  8.63 us
    ppermute x4, starting transfers between devices, exchange(): from_across = lax.ppermute(to_across, GRID, across_pairs)  2.8 us
    ppermute x1, starting transfers between devices, on_device(): arrived = lax.ppermute(theirs, GRID, mates)  2.27 us
  transfers between devices with their start and end apart: 9, of which 3 were waited for; matrix products, arithmetic and copies ran while one was open for 0% of the time, Pallas kernels for 5%

profile of v4, /device:TPU:2, one launch (start us, length us, event | category | flops | bytes accessed | tf_op | source)
XLA Modules:
  0.0 88.2 jit_solution(3908393247835138843)
XLA Ops:
  0.6 0.0 copy-start.9
  0.6 0.7 copy-done.9
  1.3 0.0 copy-start.7
  1.3 0.0 copy-start.8
  1.3 0.0 copy-start.2
  1.3 0.0 copy-start.6
  1.3 0.0 copy-start.1
  1.3 3.4 %shard_map.121 = (bf16[128,512]{1,0:T(8,128)(2,1)S(1)}, bf16[128,512]{1,0:T(8,128)(2,1)S(1)}, bf16[128,512]{1,0:T(8,128)(2,1)S(1)}, bf16[384,1024]{1,0:T(8,128)(2,1)}) custom-call(s32[2,8]{1,0:T(2,128)S(1)} %bitcast.14, bf16[1024,512]{1,0:T(8,128)(2,1)} %bitcast.7, bf16[512,512]{1,0:T(8,128)(2,1)} %weight.7, bf16[8,2,128,128]{3,2,1,0:T(8,128)(2,1)} %edges_hbm.1), custom_call_target="tpu_custom_call" | custom-call | flops 939524096 | bytes 4194304 | tf_op jit(solution)/shard_map/pallas_call | solution.py:56
  4.8 0.0 copy-start
  4.8 0.8 collective-permute-start
  5.6 5.6 %collective-permute-start.1 = (bf16[128,512]{1,0:T(8,128)(2,1)S(1)}, bf16[128,512]{1,0:T(8,128)(2,1)S(1)}, u32[]{:S(2)}, u32[]{:S(2)}) collective-permute-start(bf16[128,512]{1,0:T(8,128)(2,1)S(1)} %get-tuple-element.41), channel_id=1, source_target_pairs={{0,1},{2,3},{4,5},{6,7},{8,9},{10,11},{12,13},{14,15},{16,17},{18,... | collective-permute-start | bytes 393224 | tf_op jit(solution)/shard_map/ppermute | solution.py:226
  11.2 0.0 copy-done.7
  11.3 0.0 copy-done.8
  11.3 0.7 shard_map.122
  11.9 0.0 collective-permute-done.across
  11.9 0.3 collective-permute-done.1.mate
  12.2 0.0 copy-done.2
  12.2 0.0 copy-done.6
  12.2 0.3 shard_map.123
  12.5 0.7 collective-permute-start.2
  13.2 0.0 copy-start.4
  13.2 0.0 copy-start.5
  13.2 5.8 %collective-permute-start.3 = (bf16[128,512]{1,0:T(8,128)(2,1)S(1)}, bf16[128,512]{1,0:T(8,128)(2,1)S(1)}, u32[]{:S(2)}, u32[]{:S(2)}) collective-permute-start(bf16[128,512]{1,0:T(8,128)(2,1)S(1)} %get-tuple-element.46.own), channel_id=1, source_target_pairs={{0,1},{2,3},{4,5},{6,7},{8,9},{10,11},{12,13},{14,15},{16,17},{18,... | collective-permute-start | bytes 393224 | tf_op jit(solution)/shard_map/ppermute | solution.py:226
  19.0 0.0 copy-done.1
  19.0 0.0 copy-done
  19.0 0.9 %shard_map.124.slope = bf16[1024,512]{1,0:T(8,128)(2,1)S(1)} custom-call(bf16[1024,512]{1,0:T(8,128)(2,1)S(1)} %bitcast.8, bf16[512,512]{1,0:T(8,128)(2,1)S(1)} %copy-done.1), custom_call_target="tpu_custom_call" | custom-call | flops 536870912 | bytes 3145728 | tf_op jit(solution)/shard_map/pallas_call | solution.py:56
  20.0 0.0 collective-permute-done.2.across
  20.0 0.0 collective-permute-done.3.mate
  20.0 0.0 copy-done.4
  20.0 0.0 copy-done.5
  20.0 1.1 %shard_map.125 = (bf16[128,512]{1,0:T(8,128)(2,1)}, bf16[128,512]{1,0:T(8,128)(2,1)S(1)}, bf16[128,512]{1,0:T(8,128)(2,1)S(1)}, bf16[128,512]{1,0:T(8,128)(2,1)S(1)}) custom-call(bf16[128,512]{1,0:T(8,128)(2,1)S(1)} %collective-permute-done.2.across, bf16[128,512]{1,0:T(8,128)(2,1)S(1)} %get-tuple-element.46.own, ...), custom_call_target="tpu_custom_call" | custom-call | flops 134217728 | bytes 1048576 | tf_op jit(solution)/shard_map/pallas_call | solution.py:56
  21.1 0.7 collective-permute-start.4
  21.8 5.6 %collective-permute-start.5 = (bf16[128,512]{1,0:T(8,128)(2,1)S(1)}, bf16[128,512]{1,0:T(8,128)(2,1)S(1)}, u32[]{:S(2)}, u32[]{:S(2)}) collective-permute-start(bf16[128,512]{1,0:T(8,128)(2,1)S(1)} %get-tuple-element.55), channel_id=1, source_target_pairs={{0,1},{2,3},{4,5},{6,7},{8,9},{10,11},{12,13},{14,15},{16,17},{18,... | collective-permute-start | bytes 393224 | tf_op jit(solution)/shard_map/ppermute | solution.py:226
  27.5 0.7 shard_map.126.sorted_x
  28.2 0.0 copy-start.3
  28.2 0.0 collective-permute-done.4.across
  28.2 0.2 collective-permute-done.5.mate
  28.4 0.3 shard_map.127
  28.7 0.7 collective-permute-start.6
  29.4 6.8 %collective-permute-start.7 = (bf16[128,512]{1,0:T(8,128)(2,1)S(1)}, bf16[128,512]{1,0:T(8,128)(2,1)S(1)}, u32[]{:S(2)}, u32[]{:S(2)}) collective-permute-start(bf16[128,512]{1,0:T(8,128)(2,1)S(1)} %get-tuple-element.58.own), channel_id=1, source_target_pairs={{0,1},{2,3},{4,5},{6,7},{8,9},{10,11},{12,13},{14,15},{16,17},{18,... | collective-permute-start | bytes 393224 | tf_op jit(solution)/shard_map/ppermute | solution.py:226
  36.3 0.0 copy-done.3
  36.3 0.4 shard_map.128
  36.7 0.0 collective-permute-done.6.across
  36.7 0.5 collective-permute-done.7.mate
  37.2 1.0 %shard_map.129 = (bf16[1024,512]{1,0:T(8,128)(2,1)S(1)}, bf16[256,512]{1,0:T(8,128)(2,1)S(1)}) custom-call(bf16[128,512]{1,0:T(8,128)(2,1)S(1)} %collective-permute-done.6.across, bf16[128,512]{1,0:T(8,128)(2,1)S(1)} %get-tuple-element.58.own, bf16[128,512]{1,0:T(8,128)(2,1)S(1)} %collective-permute-done.7.mate, ...), custom_call_target="tpu_custom_call" | custom-call | flops 671088640 | bytes 4194304 | tf_op jit(solution)/shard_map/pallas_call | solution.py:56
  38.2 2.3 %collective-permute-start.8 = (bf16[256,512]{1,0:T(8,128)(2,1)S(1)}, bf16[256,512]{1,0:T(8,128)(2,1)S(1)}, u32[]{:S(2)}, u32[]{:S(2)}) collective-permute-start(bf16[256,512]{1,0:T(8,128)(2,1)S(1)} %get-tuple-element.66), channel_id=1, source_target_pairs={{0,1},{2,3},{4,5},{6,7},{8,9},{10,11},{12,13},{14,15},{16,17},{18,... | collective-permute-start | bytes 786440 | tf_op jit(solution)/shard_map/ppermute | solution.py:294
  40.5 1.5 %shard_map.130 = (f32[256,512]{1,0:T(8,128)S(1)}, bf16[1024,512]{1,0:T(8,128)(2,1)}) custom-call(bf16[512,1024]{1,0:T(8,128)(2,1)S(1)} %shard_map.126.sorted_x, bf16[1024,512]{1,0:T(8,128)(2,1)S(1)} %get-tuple-element.62.delta, bf16[512,512]{1,0:T(8,128)(2,1)S(1)} %get-tuple-element.63.weight_turned), custom_call_target="tpu_custom_call" | custom-call | flops 805306368 | bytes 4194304 | tf_op jit(solution)/shard_map/pallas_call | solution.py:56
  41.9 0.0 collective-permute-done.8
  42.0 0.1 add_convert_fusion
  42.0 0.1 reshape.9
  42.1 36.7 %all_to_all.10 = bf16[64,4,512]{2,1,0:T(4,128)(2,1)S(1)} all-to-all(bf16[64,4,512]{2,1,0:T(4,128)(2,1)S(1)} %reshape.9), channel_id=1, replica_groups=mesh['ens'=4,'y'=8,'z'=8,'core'=2] {'y','z'}, dimensions={0} | all-to-all | bytes 524288 | tf_op jit(solution)/shard_map/all_to_all | solution.py:304
  78.8 0.1 convert_reduce_fusion
  79.0 8.6 %all_to_all.11 = f32[4,4,512]{2,1,0:T(4,128)S(1)} all-to-all(f32[4,4,512]{2,1,0:T(4,128)S(1)} %broadcast_in_dim.11), channel_id=1, replica_groups=mesh['ens'=4,'y'=8,'z'=8,'core'=2] {'ens'}, dimensions={0} | all-to-all | bytes 65536 | tf_op jit(solution)/shard_map/all_to_all | solution.py:308
  87.6 0.6 reduce_sum.19
  (2 shorter events, 0.0 us)
Async XLA Ops:
  0.6 0.7 copy-start.9
  1.3 9.9 %copy-start.7 = (bf16[1,2,128,128]{3,2,1,0:T(8,128)(2,1)S(1)}, bf16[1,2,128,128]{3,2,1,0:T(8,128)(2,1)}, u32[]{:S(2)}) copy-start(bf16[1,2,128,128]{3,2,1,0:T(8,128)(2,1)} %param.15) | copy-start | bytes 196612
  1.3 9.9 %copy-start.8 = (s32[1,2]{1,0:T(1,128)S(1)}, s32[1,2]{1,0:T(1,128)}, u32[]{:S(2)}) copy-start(s32[1,2]{1,0:T(1,128)} %sources) | copy-start | bytes 28
  1.3 10.9 %copy-start.2 = (bf16[512,512]{1,0:T(8,128)(2,1)S(1)}, bf16[512,512]{1,0:T(8,128)(2,1)}, u32[]{:S(2)}) copy-start(bf16[512,512]{1,0:T(8,128)(2,1)} %weight.6) | copy-start | bytes 1572868
  1.3 10.9 %copy-start.6 = (bf16[1,128,512]{2,1,0:T(8,128)(2,1)S(1)}, bf16[1,128,512]{2,1,0:T(8,128)(2,1)}, u32[]{:S(2)}) copy-start(bf16[1,128,512]{2,1,0:T(8,128)(2,1)} %param.11) | copy-start | bytes 393220
  1.3 17.7 %copy-start.1 = (bf16[512,512]{1,0:T(8,128)(2,1)S(1)}, bf16[512,512]{1,0:T(8,128)(2,1)}, u32[]{:S(2)}) copy-start(bf16[512,512]{1,0:T(8,128)(2,1)} %weight.7) | copy-start | bytes 1572868
  4.8 14.2 %copy-start = (bf16[1,1024,512]{2,1,0:T(8,128)(2,1)S(1)}, bf16[1,1024,512]{2,1,0:T(8,128)(2,1)}, u32[]{:S(2)}) copy-start(bf16[1,1024,512]{2,1,0:T(8,128)(2,1)} %param.10) | copy-start | bytes 3145732
  4.8 7.1 %collective-permute-start = (bf16[128,512]{1,0:T(8,128)(2,1)S(1)}, bf16[128,512]{1,0:T(8,128)(2,1)S(1)}, u32[]{:S(2)}, u32[]{:S(2)}) collective-permute-start(bf16[128,512]{1,0:T(8,128)(2,1)S(1)} %get-tuple-element.35), channel_id=1, source_target_pairs={{1,2},{3,4},{5,6},{7,8},{9,10},{11,12},{13,14},{15,16},{17,18},{19... | collective-permute-start | bytes 393224 | tf_op jit(solution)/shard_map/ppermute | solution.py:227
  5.6 6.6 %collective-permute-start.1 = (bf16[128,512]{1,0:T(8,128)(2,1)S(1)}, bf16[128,512]{1,0:T(8,128)(2,1)S(1)}, u32[]{:S(2)}, u32[]{:S(2)}) collective-permute-start(bf16[128,512]{1,0:T(8,128)(2,1)S(1)} %get-tuple-element.41), channel_id=1, source_target_pairs={{0,1},{2,3},{4,5},{6,7},{8,9},{10,11},{12,13},{14,15},{16,17},{18,... | collective-permute-start | bytes 393224 | tf_op jit(solution)/shard_map/ppermute | solution.py:226
  12.5 7.4 %collective-permute-start.2 = (bf16[128,512]{1,0:T(8,128)(2,1)S(1)}, bf16[128,512]{1,0:T(8,128)(2,1)S(1)}, u32[]{:S(2)}, u32[]{:S(2)}) collective-permute-start(bf16[128,512]{1,0:T(8,128)(2,1)S(1)} %get-tuple-element.42), channel_id=1, source_target_pairs={{1,2},{3,4},{5,6},{7,8},{9,10},{11,12},{13,14},{15,16},{17,18},{19... | collective-permute-start | bytes 393224 | tf_op jit(solution)/shard_map/ppermute | solution.py:227
  13.2 6.8 %copy-start.4 = (bf16[1,128,512]{2,1,0:T(8,128)(2,1)S(1)}, bf16[1,128,512]{2,1,0:T(8,128)(2,1)}, u32[]{:S(2)}) copy-start(bf16[1,128,512]{2,1,0:T(8,128)(2,1)} %param.12) | copy-start | bytes 393220
  13.2 6.8 %copy-start.5 = (bf16[512,512]{1,0:T(8,128)(2,1)S(1)}, bf16[512,512]{1,0:T(8,128)(2,1)}, u32[]{:S(2)}) copy-start(bf16[512,512]{1,0:T(8,128)(2,1)} %weight.5) | copy-start | bytes 1572868
  13.2 6.7 %collective-permute-start.3 = (bf16[128,512]{1,0:T(8,128)(2,1)S(1)}, bf16[128,512]{1,0:T(8,128)(2,1)S(1)}, u32[]{:S(2)}, u32[]{:S(2)}) collective-permute-start(bf16[128,512]{1,0:T(8,128)(2,1)S(1)} %get-tuple-element.46.own), channel_id=1, source_target_pairs={{0,1},{2,3},{4,5},{6,7},{8,9},{10,11},{12,13},{14,15},{16,17},{18,... | collective-permute-start | bytes 393224 | tf_op jit(solution)/shard_map/ppermute | solution.py:226
  21.1 7.1 %collective-permute-start.4 = (bf16[128,512]{1,0:T(8,128)(2,1)S(1)}, bf16[128,512]{1,0:T(8,128)(2,1)S(1)}, u32[]{:S(2)}, u32[]{:S(2)}) collective-permute-start(bf16[128,512]{1,0:T(8,128)(2,1)S(1)} %get-tuple-element.53), channel_id=1, source_target_pairs={{1,2},{3,4},{5,6},{7,8},{9,10},{11,12},{13,14},{15,16},{17,18},{19... | collective-permute-start | bytes 393224 | tf_op jit(solution)/shard_map/ppermute | solution.py:227
  21.8 6.6 %collective-permute-start.5 = (bf16[128,512]{1,0:T(8,128)(2,1)S(1)}, bf16[128,512]{1,0:T(8,128)(2,1)S(1)}, u32[]{:S(2)}, u32[]{:S(2)}) collective-permute-start(bf16[128,512]{1,0:T(8,128)(2,1)S(1)} %get-tuple-element.55), channel_id=1, source_target_pairs={{0,1},{2,3},{4,5},{6,7},{8,9},{10,11},{12,13},{14,15},{16,17},{18,... | collective-permute-start | bytes 393224 | tf_op jit(solution)/shard_map/ppermute | solution.py:226
  28.2 8.1 %copy-start.3 = (bf16[384,1024]{1,0:T(8,128)(2,1)S(1)}, bf16[384,1024]{1,0:T(8,128)(2,1)}, u32[]{:S(2)}) copy-start(bf16[384,1024]{1,0:T(8,128)(2,1)} %get-tuple-element.59.laid) | copy-start | bytes 2359300
  28.7 7.9 %collective-permute-start.6 = (bf16[128,512]{1,0:T(8,128)(2,1)S(1)}, bf16[128,512]{1,0:T(8,128)(2,1)S(1)}, u32[]{:S(2)}, u32[]{:S(2)}) collective-permute-start(bf16[128,512]{1,0:T(8,128)(2,1)S(1)} %get-tuple-element.57), channel_id=1, source_target_pairs={{1,2},{3,4},{5,6},{7,8},{9,10},{11,12},{13,14},{15,16},{17,18},{19... | collective-permute-start | bytes 393224 | tf_op jit(solution)/shard_map/ppermute | solution.py:227
  29.4 7.8 %collective-permute-start.7 = (bf16[128,512]{1,0:T(8,128)(2,1)S(1)}, bf16[128,512]{1,0:T(8,128)(2,1)S(1)}, u32[]{:S(2)}, u32[]{:S(2)}) collective-permute-start(bf16[128,512]{1,0:T(8,128)(2,1)S(1)} %get-tuple-element.58.own), channel_id=1, source_target_pairs={{0,1},{2,3},{4,5},{6,7},{8,9},{10,11},{12,13},{14,15},{16,17},{18,... | collective-permute-start | bytes 393224 | tf_op jit(solution)/shard_map/ppermute | solution.py:226
  38.2 3.7 %collective-permute-start.8 = (bf16[256,512]{1,0:T(8,128)(2,1)S(1)}, bf16[256,512]{1,0:T(8,128)(2,1)S(1)}, u32[]{:S(2)}, u32[]{:S(2)}) collective-permute-start(bf16[256,512]{1,0:T(8,128)(2,1)S(1)} %get-tuple-element.66), channel_id=1, source_target_pairs={{0,1},{2,3},{4,5},{6,7},{8,9},{10,11},{12,13},{14,15},{16,17},{18,... | collective-permute-start | bytes 786440 | tf_op jit(solution)/shard_map/ppermute | solution.py:294

commit v5 on v4

--- a/solution.py
+++ b/solution.py
@@ -71,8 +71,8 @@
 
 
 def encode_kernel(
-    targets, x_hbm, weight_hbm, edges_hbm, across, own, mate, laid_hbm,
-    x, weight, edges, messages, laid, arrived, left,
+    targets, x_hbm, weight_hbm, edges_hbm, across, own, mate,
+    x, weight, edges, messages, laid, arrived,
 ):
     blocks, picks, rows, cols = edges.shape
     nodes = x.shape[0]
@@ -103,8 +103,6 @@
             at = pl.ds(pl.multiple_of(slot_of(targets[k, b]) * rows, rows), rows)
             laid[at, b * cols : (b + 1) * cols] = edges[b, k]
     encode(1)
-    laid_out = pltpu.make_async_copy(laid, laid_hbm, left)
-    laid_out.start()
     x_in[2].wait()
     x_in[3].wait()
     encode(2)
@@ -112,7 +110,6 @@
     across[...] = dot(laid[:rows, :], messages[...], 1, 0).astype(BF)
     own[...] = dot(laid[rows : 2 * rows, :], messages[...], 1, 0).astype(BF)
     mate[...] = dot(laid[2 * rows :, :], messages[...], 1, 0).astype(BF)
-    laid_out.wait()
 
 
 def slope_kernel(x, weight, slope):
@@ -122,8 +119,13 @@
         slope[at, :] = silu_and_slope(dot(x[at, :], weight[...], 1, 0))[1].astype(BF)
 
 
-def turn_kernel(laid, weight, turned, weight_turned):
-    turned[...] = laid[...].T
+def turn_kernel(targets, edges, weight, turned, weight_turned):
+    blocks, picks, rows, cols = edges.shape
+    turned[...] = jnp.zeros_like(turned)
+    for b in range(blocks):
+        for k in range(picks):
+            at = pl.ds(pl.multiple_of(slot_of(targets[k, b]) * rows, rows), rows)
+            turned[b * cols : (b + 1) * cols, at] = edges[b, k].T
     weight_turned[...] = weight[...].T
 
 
@@ -231,20 +233,20 @@
     grid_x = grid_latent[0]
     block = ((rows, width), BF)
     near = ((3 * rows, width), BF)
-    to_across, own, to_mate, laid = call(
+    to_across, own, to_mate = call(
         encode_kernel,
-        [block, block, block, ((3 * rows, nodes), BF, pltpu.HBM)],
+        [block, block, block],
         [
             (grid_x.shape, BF), (encode_weight.shape, BF), (edge_weights.shape, BF),
             ((nodes, width), BF), ((3 * rows, nodes), BF),
-            pltpu.SemaphoreType.DMA((6,)), pltpu.SemaphoreType.DMA,
+            pltpu.SemaphoreType.DMA((6,)),
         ],
         2 * nodes * width * (width + 3 * rows), 4 << 20,
         edge_targets.T, grid_x, encode_weight, edge_weights,
         copied=True,
     )
     across, mate = exchange(to_across, to_mate)
-    sources, _ = lax.optimization_barrier((mesh_sources, laid))
+    sources, _ = lax.optimization_barrier((mesh_sources, own))
     mixing, mixing_turned = call(
         mix_kernel, [((rows, 3 * rows), BF), ((3 * rows, rows), BF)], [], 0, 1 << 18,
         sources, mesh_weights[0],
@@ -256,14 +258,17 @@
         across, own, mate, mesh_latent[0], aggregate_weight,
     )
     across, mate = exchange(again, updated)
-    later, grid_y, weight, _ = lax.optimization_barrier((laid, grid_x, encode_weight, updated))
+    targets, edges, grid_y, weight, _ = lax.optimization_barrier(
+        (edge_targets.T, edge_weights, grid_x, encode_weight, updated)
+    )
     slope = call(
         slope_kernel, [((nodes, width), BF)], [],
         2 * nodes * width * width, 3 << 20,
         grid_y, weight,
     )
     turned, weight_turned = call(
-        turn_kernel, [((nodes, 3 * rows), BF), ((width, width), BF)], [], 0, 2 << 20, later, weight
+        turn_kernel, [((nodes, 3 * rows), BF), ((width, width), BF)], [], 0, 2 << 20,
+        targets, edges, weight,
     )
     updated, slope = lax.optimization_barrier((updated, slope))
     result, to_across, own, to_mate = call(

time: 88.7 us -> 88.7 us (level)
  no operation moved by 1% of the time
where the time goes in v5:
time: 88.7 us; the launch traced here: 88.2 us
  blocking collectives  45.3 us (51%)
  starting transfers between devices  28.9 us (33%)
  Pallas kernels  10.8 us (12%)
  between operations  0.94 us (1%)
    all_to_all x1, blocking collectives, on_device(): parts = lax.all_to_all(pair.reshape(chips, share, width), ('y', 'z'), 0, 0)  36.7 us
    ppermute x4, starting transfers between devices, exchange(): from_mate = lax.ppermute(to_mate, GRID, mates)  23.9 us
    pallas_call x10, Pallas kernels, call(): pl.pallas_call(kernel, out_shape=shapes[0] if single else shapes, in_spec...  10.8 us
    all_to_all x1, blocking collectives, on_device(): final = lax.all_to_all(summed, 'ens', 0, 0).sum(0)  8.62 us
    ppermute x4, starting transfers between devices, exchange(): from_across = lax.ppermute(to_across, GRID, across_pairs)  2.8 us
    ppermute x1, starting transfers between devices, on_device(): arrived = lax.ppermute(theirs, GRID, mates)  2.26 us
  transfers between devices with their start and end apart: 9, of which 3 were waited for; matrix products, arithmetic and copies ran while one was open for 0% of the time, Pallas kernels for 5%

profile of v5, /device:TPU:2, one launch (start us, length us, event | category | flops | bytes accessed | tf_op | source)
XLA Modules:
  0.0 88.2 jit_solution(11576827942439015789)
XLA Ops:
  0.6 0.0 copy-start.8
  0.6 0.7 copy-done.8
  1.3 0.0 copy-start.7
  1.3 0.0 copy-start.9
  1.3 0.0 copy-start.2
  1.3 0.0 copy-start.6
  1.3 0.0 copy-start.1
  1.3 3.5 %shard_map.121 = (bf16[128,512]{1,0:T(8,128)(2,1)S(1)}, bf16[128,512]{1,0:T(8,128)(2,1)S(1)}, bf16[128,512]{1,0:T(8,128)(2,1)S(1)}) custom-call(s32[2,8]{1,0:T(2,128)S(1)} %bitcast.14, bf16[1024,512]{1,0:T(8,128)(2,1)} %bitcast.7, bf16[512,512]{1,0:T(8,128)(2,1)} %weight.7, bf16[8,2,128,128]{3,2,1,0:T(8,128)(2,1)} %edges), custom_call_target="tpu_custom_call" | custom-call | flops 939524096 | bytes 4194304 | tf_op jit(solution)/shard_map/pallas_call | solution.py:56
  4.8 0.0 copy-start
  4.8 0.8 collective-permute-start
  5.6 5.6 %collective-permute-start.1 = (bf16[128,512]{1,0:T(8,128)(2,1)S(1)}, bf16[128,512]{1,0:T(8,128)(2,1)S(1)}, u32[]{:S(2)}, u32[]{:S(2)}) collective-permute-start(bf16[128,512]{1,0:T(8,128)(2,1)S(1)} %get-tuple-element.40), channel_id=1, source_target_pairs={{0,1},{2,3},{4,5},{6,7},{8,9},{10,11},{12,13},{14,15},{16,17},{18,... | collective-permute-start | bytes 393224 | tf_op jit(solution)/shard_map/ppermute | solution.py:228
  11.3 0.0 copy-done.7
  11.3 0.0 copy-done.9
  11.3 0.7 shard_map.122
  12.0 0.0 collective-permute-done.across
  12.0 0.3 collective-permute-done.1.mate
  12.2 0.0 copy-done.2
  12.2 0.0 copy-done.6
  12.2 0.3 shard_map.123
  12.6 0.7 collective-permute-start.2
  13.2 0.0 copy-start.3
  13.2 0.0 copy-start.5
  13.3 5.8 %collective-permute-start.3 = (bf16[128,512]{1,0:T(8,128)(2,1)S(1)}, bf16[128,512]{1,0:T(8,128)(2,1)S(1)}, u32[]{:S(2)}, u32[]{:S(2)}) collective-permute-start(bf16[128,512]{1,0:T(8,128)(2,1)S(1)} %get-tuple-element.45.own), channel_id=1, source_target_pairs={{0,1},{2,3},{4,5},{6,7},{8,9},{10,11},{12,13},{14,15},{16,17},{18,... | collective-permute-start | bytes 393224 | tf_op jit(solution)/shard_map/ppermute | solution.py:228
  19.0 0.0 copy-done.1
  19.0 0.0 copy-done
  19.1 0.9 %shard_map.124.slope = bf16[1024,512]{1,0:T(8,128)(2,1)S(1)} custom-call(bf16[1024,512]{1,0:T(8,128)(2,1)S(1)} %bitcast.8, bf16[512,512]{1,0:T(8,128)(2,1)S(1)} %copy-done.1), custom_call_target="tpu_custom_call" | custom-call | flops 536870912 | bytes 3145728 | tf_op jit(solution)/shard_map/pallas_call | solution.py:56
  20.0 0.0 collective-permute-done.2.across
  20.0 0.0 collective-permute-done.3.mate
  20.0 0.0 copy-done.3
  20.0 0.0 copy-done.5
  20.0 1.1 %shard_map.125 = (bf16[128,512]{1,0:T(8,128)(2,1)}, bf16[128,512]{1,0:T(8,128)(2,1)S(1)}, bf16[128,512]{1,0:T(8,128)(2,1)S(1)}, bf16[128,512]{1,0:T(8,128)(2,1)S(1)}) custom-call(bf16[128,512]{1,0:T(8,128)(2,1)S(1)} %collective-permute-done.2.across, bf16[128,512]{1,0:T(8,128)(2,1)S(1)} %get-tuple-element.45.own, ...), custom_call_target="tpu_custom_call" | custom-call | flops 134217728 | bytes 1048576 | tf_op jit(solution)/shard_map/pallas_call | solution.py:56
  21.2 0.7 collective-permute-start.4
  21.8 5.6 %collective-permute-start.5 = (bf16[128,512]{1,0:T(8,128)(2,1)S(1)}, bf16[128,512]{1,0:T(8,128)(2,1)S(1)}, u32[]{:S(2)}, u32[]{:S(2)}) collective-permute-start(bf16[128,512]{1,0:T(8,128)(2,1)S(1)} %get-tuple-element.54), channel_id=1, source_target_pairs={{0,1},{2,3},{4,5},{6,7},{8,9},{10,11},{12,13},{14,15},{16,17},{18,... | collective-permute-start | bytes 393224 | tf_op jit(solution)/shard_map/ppermute | solution.py:228
  27.5 0.7 shard_map.126.sorted_x
  28.2 0.0 collective-permute-done.4.across
  28.2 0.2 collective-permute-done.5.mate
  28.4 0.0 copy-start.4
  28.4 0.3 shard_map.127
  28.8 0.7 collective-permute-start.6
  29.4 6.8 %collective-permute-start.7 = (bf16[128,512]{1,0:T(8,128)(2,1)S(1)}, bf16[128,512]{1,0:T(8,128)(2,1)S(1)}, u32[]{:S(2)}, u32[]{:S(2)}) collective-permute-start(bf16[128,512]{1,0:T(8,128)(2,1)S(1)} %get-tuple-element.57.own), channel_id=1, source_target_pairs={{0,1},{2,3},{4,5},{6,7},{8,9},{10,11},{12,13},{14,15},{16,17},{18,... | collective-permute-start | bytes 393224 | tf_op jit(solution)/shard_map/ppermute | solution.py:228
  36.3 0.0 copy-done.4
  36.3 0.9 shard_map.128
  37.2 0.0 collective-permute-done.6.across
  37.2 0.1 collective-permute-done.7.mate
  37.2 1.0 %shard_map.129 = (bf16[1024,512]{1,0:T(8,128)(2,1)S(1)}, bf16[256,512]{1,0:T(8,128)(2,1)S(1)}) custom-call(bf16[128,512]{1,0:T(8,128)(2,1)S(1)} %collective-permute-done.6.across, bf16[128,512]{1,0:T(8,128)(2,1)S(1)} %get-tuple-element.57.own, bf16[128,512]{1,0:T(8,128)(2,1)S(1)} %collective-permute-done.7.mate, ...), custom_call_target="tpu_custom_call" | custom-call | flops 671088640 | bytes 4194304 | tf_op jit(solution)/shard_map/pallas_call | solution.py:56
  38.2 2.3 %collective-permute-start.8 = (bf16[256,512]{1,0:T(8,128)(2,1)S(1)}, bf16[256,512]{1,0:T(8,128)(2,1)S(1)}, u32[]{:S(2)}, u32[]{:S(2)}) collective-permute-start(bf16[256,512]{1,0:T(8,128)(2,1)S(1)} %get-tuple-element.66), channel_id=1, source_target_pairs={{0,1},{2,3},{4,5},{6,7},{8,9},{10,11},{12,13},{14,15},{16,17},{18,... | collective-permute-start | bytes 786440 | tf_op jit(solution)/shard_map/ppermute | solution.py:299
  40.5 1.4 %shard_map.130 = (f32[256,512]{1,0:T(8,128)S(1)}, bf16[1024,512]{1,0:T(8,128)(2,1)}) custom-call(bf16[512,1024]{1,0:T(8,128)(2,1)S(1)} %shard_map.126.sorted_x, bf16[1024,512]{1,0:T(8,128)(2,1)S(1)} %get-tuple-element.62.delta, bf16[512,512]{1,0:T(8,128)(2,1)S(1)} %get-tuple-element.63.weight_turned), custom_call_target="tpu_custom_call" | custom-call | flops 805306368 | bytes 4194304 | tf_op jit(solution)/shard_map/pallas_call | solution.py:56
  42.0 0.0 collective-permute-done.8
  42.0 0.1 add_convert_fusion
  42.0 0.1 reshape.9
  42.1 36.7 %all_to_all.10 = bf16[64,4,512]{2,1,0:T(4,128)(2,1)S(1)} all-to-all(bf16[64,4,512]{2,1,0:T(4,128)(2,1)S(1)} %reshape.9), channel_id=1, replica_groups=mesh['ens'=4,'y'=8,'z'=8,'core'=2] {'y','z'}, dimensions={0} | all-to-all | bytes 524288 | tf_op jit(solution)/shard_map/all_to_all | solution.py:309
  78.8 0.1 convert_reduce_fusion
  79.0 8.6 %all_to_all.11 = f32[4,4,512]{2,1,0:T(4,128)S(1)} all-to-all(f32[4,4,512]{2,1,0:T(4,128)S(1)} %broadcast_in_dim.11), channel_id=1, replica_groups=mesh['ens'=4,'y'=8,'z'=8,'core'=2] {'ens'}, dimensions={0} | all-to-all | bytes 65536 | tf_op jit(solution)/shard_map/all_to_all | solution.py:313
  87.6 0.6 reduce_sum.19
  (2 shorter events, 0.0 us)
Async XLA Ops:
  0.6 0.7 copy-start.8
  1.3 10.0 %copy-start.7 = (bf16[1,2,128,128]{3,2,1,0:T(8,128)(2,1)S(1)}, bf16[1,2,128,128]{3,2,1,0:T(8,128)(2,1)}, u32[]{:S(2)}) copy-start(bf16[1,2,128,128]{3,2,1,0:T(8,128)(2,1)} %param.15) | copy-start | bytes 196612
  1.3 10.0 %copy-start.9 = (s32[1,2]{1,0:T(1,128)S(1)}, s32[1,2]{1,0:T(1,128)}, u32[]{:S(2)}) copy-start(s32[1,2]{1,0:T(1,128)} %sources) | copy-start | bytes 28
  1.3 10.9 %copy-start.2 = (bf16[512,512]{1,0:T(8,128)(2,1)S(1)}, bf16[512,512]{1,0:T(8,128)(2,1)}, u32[]{:S(2)}) copy-start(bf16[512,512]{1,0:T(8,128)(2,1)} %weight.6) | copy-start | bytes 1572868
  1.3 10.9 %copy-start.6 = (bf16[1,128,512]{2,1,0:T(8,128)(2,1)S(1)}, bf16[1,128,512]{2,1,0:T(8,128)(2,1)}, u32[]{:S(2)}) copy-start(bf16[1,128,512]{2,1,0:T(8,128)(2,1)} %param.11) | copy-start | bytes 393220
  1.3 17.7 %copy-start.1 = (bf16[512,512]{1,0:T(8,128)(2,1)S(1)}, bf16[512,512]{1,0:T(8,128)(2,1)}, u32[]{:S(2)}) copy-start(bf16[512,512]{1,0:T(8,128)(2,1)} %weight.7) | copy-start | bytes 1572868
  4.8 14.2 %copy-start = (bf16[1,1024,512]{2,1,0:T(8,128)(2,1)S(1)}, bf16[1,1024,512]{2,1,0:T(8,128)(2,1)}, u32[]{:S(2)}) copy-start(bf16[1,1024,512]{2,1,0:T(8,128)(2,1)} %param.10) | copy-start | bytes 3145732
  4.8 7.1 %collective-permute-start = (bf16[128,512]{1,0:T(8,128)(2,1)S(1)}, bf16[128,512]{1,0:T(8,128)(2,1)S(1)}, u32[]{:S(2)}, u32[]{:S(2)}) collective-permute-start(bf16[128,512]{1,0:T(8,128)(2,1)S(1)} %get-tuple-element.35), channel_id=1, source_target_pairs={{1,2},{3,4},{5,6},{7,8},{9,10},{11,12},{13,14},{15,16},{17,18},{19... | collective-permute-start | bytes 393224 | tf_op jit(solution)/shard_map/ppermute | solution.py:229
  5.6 6.6 %collective-permute-start.1 = (bf16[128,512]{1,0:T(8,128)(2,1)S(1)}, bf16[128,512]{1,0:T(8,128)(2,1)S(1)}, u32[]{:S(2)}, u32[]{:S(2)}) collective-permute-start(bf16[128,512]{1,0:T(8,128)(2,1)S(1)} %get-tuple-element.40), channel_id=1, source_target_pairs={{0,1},{2,3},{4,5},{6,7},{8,9},{10,11},{12,13},{14,15},{16,17},{18,... | collective-permute-start | bytes 393224 | tf_op jit(solution)/shard_map/ppermute | solution.py:228
  12.6 7.4 %collective-permute-start.2 = (bf16[128,512]{1,0:T(8,128)(2,1)S(1)}, bf16[128,512]{1,0:T(8,128)(2,1)S(1)}, u32[]{:S(2)}, u32[]{:S(2)}) collective-permute-start(bf16[128,512]{1,0:T(8,128)(2,1)S(1)} %get-tuple-element.41), channel_id=1, source_target_pairs={{1,2},{3,4},{5,6},{7,8},{9,10},{11,12},{13,14},{15,16},{17,18},{19... | collective-permute-start | bytes 393224 | tf_op jit(solution)/shard_map/ppermute | solution.py:229
  13.2 6.8 %copy-start.3 = (bf16[1,128,512]{2,1,0:T(8,128)(2,1)S(1)}, bf16[1,128,512]{2,1,0:T(8,128)(2,1)}, u32[]{:S(2)}) copy-start(bf16[1,128,512]{2,1,0:T(8,128)(2,1)} %param.12) | copy-start | bytes 393220
  13.2 6.8 %copy-start.5 = (bf16[512,512]{1,0:T(8,128)(2,1)S(1)}, bf16[512,512]{1,0:T(8,128)(2,1)}, u32[]{:S(2)}) copy-start(bf16[512,512]{1,0:T(8,128)(2,1)} %weight.5) | copy-start | bytes 1572868
  13.3 6.7 %collective-permute-start.3 = (bf16[128,512]{1,0:T(8,128)(2,1)S(1)}, bf16[128,512]{1,0:T(8,128)(2,1)S(1)}, u32[]{:S(2)}, u32[]{:S(2)}) collective-permute-start(bf16[128,512]{1,0:T(8,128)(2,1)S(1)} %get-tuple-element.45.own), channel_id=1, source_target_pairs={{0,1},{2,3},{4,5},{6,7},{8,9},{10,11},{12,13},{14,15},{16,17},{18,... | collective-permute-start | bytes 393224 | tf_op jit(solution)/shard_map/ppermute | solution.py:228
  21.2 7.1 %collective-permute-start.4 = (bf16[128,512]{1,0:T(8,128)(2,1)S(1)}, bf16[128,512]{1,0:T(8,128)(2,1)S(1)}, u32[]{:S(2)}, u32[]{:S(2)}) collective-permute-start(bf16[128,512]{1,0:T(8,128)(2,1)S(1)} %get-tuple-element.52), channel_id=1, source_target_pairs={{1,2},{3,4},{5,6},{7,8},{9,10},{11,12},{13,14},{15,16},{17,18},{19... | collective-permute-start | bytes 393224 | tf_op jit(solution)/shard_map/ppermute | solution.py:229
  21.8 6.6 %collective-permute-start.5 = (bf16[128,512]{1,0:T(8,128)(2,1)S(1)}, bf16[128,512]{1,0:T(8,128)(2,1)S(1)}, u32[]{:S(2)}, u32[]{:S(2)}) collective-permute-start(bf16[128,512]{1,0:T(8,128)(2,1)S(1)} %get-tuple-element.54), channel_id=1, source_target_pairs={{0,1},{2,3},{4,5},{6,7},{8,9},{10,11},{12,13},{14,15},{16,17},{18,... | collective-permute-start | bytes 393224 | tf_op jit(solution)/shard_map/ppermute | solution.py:228
  28.4 7.8 %copy-start.4 = (bf16[8,2,128,128]{3,2,1,0:T(8,128)(2,1)S(1)}, bf16[8,2,128,128]{3,2,1,0:T(8,128)(2,1)}, u32[]{:S(2)}) copy-start(bf16[8,2,128,128]{3,2,1,0:T(8,128)(2,1)} %edges) | copy-start | bytes 1572868
  28.8 8.4 %collective-permute-start.6 = (bf16[128,512]{1,0:T(8,128)(2,1)S(1)}, bf16[128,512]{1,0:T(8,128)(2,1)S(1)}, u32[]{:S(2)}, u32[]{:S(2)}) collective-permute-start(bf16[128,512]{1,0:T(8,128)(2,1)S(1)} %get-tuple-element.56), channel_id=1, source_target_pairs={{1,2},{3,4},{5,6},{7,8},{9,10},{11,12},{13,14},{15,16},{17,18},{19... | collective-permute-start | bytes 393224 | tf_op jit(solution)/shard_map/ppermute | solution.py:229
  29.4 7.8 %collective-permute-start.7 = (bf16[128,512]{1,0:T(8,128)(2,1)S(1)}, bf16[128,512]{1,0:T(8,128)(2,1)S(1)}, u32[]{:S(2)}, u32[]{:S(2)}) collective-permute-start(bf16[128,512]{1,0:T(8,128)(2,1)S(1)} %get-tuple-element.57.own), channel_id=1, source_target_pairs={{0,1},{2,3},{4,5},{6,7},{8,9},{10,11},{12,13},{14,15},{16,17},{18,... | collective-permute-start | bytes 393224 | tf_op jit(solution)/shard_map/ppermute | solution.py:228
  38.2 3.7 %collective-permute-start.8 = (bf16[256,512]{1,0:T(8,128)(2,1)S(1)}, bf16[256,512]{1,0:T(8,128)(2,1)S(1)}, u32[]{:S(2)}, u32[]{:S(2)}) collective-permute-start(bf16[256,512]{1,0:T(8,128)(2,1)S(1)} %get-tuple-element.66), channel_id=1, source_target_pairs={{0,1},{2,3},{4,5},{6,7},{8,9},{10,11},{12,13},{14,15},{16,17},{18,... | collective-permute-start | bytes 786440 | tf_op jit(solution)/shard_map/ppermute | solution.py:299

commit v6 on v5

--- a/solution.py
+++ b/solution.py
@@ -152,13 +152,14 @@
     again[...] = fresh
 
 
-def mix_kernel(sources, mixing, laid, turned):
+def mix_kernel(sources, mixing, weight, laid, turned, weight_turned):
     rows = mixing.shape[1]
     laid[...] = jnp.zeros_like(laid)
     for k in range(mixing.shape[0]):
         at = pl.ds(pl.multiple_of(slot_of(sources[0, k]) * rows, rows), rows)
         laid[:, at] = mixing[k]
     turned[...] = laid[...].T
+    weight_turned[...] = weight[...].T
 
 
 def process_kernel(
@@ -177,10 +178,10 @@
     to_across[...], to_own[...], to_mate[...] = pushed[:rows], pushed[rows : 2 * rows], pushed[2 * rows :]
 
 
-def return_kernel(across, own, mate, cotangent, slope, weight, grad, again):
+def return_kernel(across, own, mate, cotangent, slope, weight_turned, grad, again):
     total = cotangent[...].astype(F32) + own[...].astype(F32)
     total = total + across[...].astype(F32) + mate[...].astype(F32)
-    fresh = dot((total * slope[...]).astype(BF), weight[...], 1, 1).astype(BF)
+    fresh = dot((total * slope[...]).astype(BF), weight_turned[...], 1, 0).astype(BF)
     grad[...] = fresh
     again[...] = fresh
 
@@ -247,9 +248,10 @@
     )
     across, mate = exchange(to_across, to_mate)
     sources, _ = lax.optimization_barrier((mesh_sources, own))
-    mixing, mixing_turned = call(
-        mix_kernel, [((rows, 3 * rows), BF), ((3 * rows, rows), BF)], [], 0, 1 << 18,
-        sources, mesh_weights[0],
+    mixing, mixing_turned, aggregate_turned = call(
+        mix_kernel, [((rows, 3 * rows), BF), ((3 * rows, rows), BF), ((width, width), BF)], [],
+        0, 1 << 20,
+        sources, mesh_weights[0], aggregate_weight,
     )
     own, mixing = lax.optimization_barrier((own, mixing))
     updated, again, mesh_slope = call(
@@ -288,7 +290,7 @@
     agg_grad, again = call(
         return_kernel, [block, block], [],
         2 * rows * width * width, 1 << 20,
-        across, own, mate, cotangent[0], mesh_slope, aggregate_weight,
+        across, own, mate, cotangent[0], mesh_slope, aggregate_turned,
     )
     across, mate = exchange(again, agg_grad)
     enc_delta, theirs = call(

time: 88.7 us -> 88.6 us (level)
  no operation moved by 1% of the time
where the time goes in v6:
time: 88.6 us; the launch traced here: 88.2 us
  blocking collectives  45.3 us (51%)
  starting transfers between devices  29 us (33%)
  Pallas kernels  10.9 us (12%)
  between operations  0.92 us (1%)
    all_to_all x1, blocking collectives, on_device(): parts = lax.all_to_all(pair.reshape(chips, share, width), ('y', 'z'), 0, 0)  36.7 us
    ppermute x4, starting transfers between devices, exchange(): from_mate = lax.ppermute(to_mate, GRID, mates)  23.9 us
    pallas_call x10, Pallas kernels, call(): pl.pallas_call(kernel, out_shape=shapes[0] if single else shapes, in_spec...  10.9 us
    all_to_all x1, blocking collectives, on_device(): final = lax.all_to_all(summed, 'ens', 0, 0).sum(0)  8.63 us
    ppermute x4, starting transfers between devices, exchange(): from_across = lax.ppermute(to_across, GRID, across_pairs)  2.8 us
    ppermute x1, starting transfers between devices, on_device(): arrived = lax.ppermute(theirs, GRID, mates)  2.27 us
  transfers between devices with their start and end apart: 9, of which 3 were waited for; matrix products, arithmetic and copies ran while one was open for 0% of the time, Pallas kernels for 5%

profile of v6, /device:TPU:2, one launch (start us, length us, event | category | flops | bytes accessed | tf_op | source)
XLA Modules:
  0.0 88.2 jit_solution(5348791831865935405)
XLA Ops:
  0.6 0.0 copy-start.8
  0.6 0.7 copy-done.8
  1.3 0.0 copy-start.2
  1.3 0.0 copy-start.7
  1.3 0.0 copy-start.9
  1.3 0.0 copy-start.6
  1.3 3.5 %shard_map.121 = (bf16[128,512]{1,0:T(8,128)(2,1)S(1)}, bf16[128,512]{1,0:T(8,128)(2,1)S(1)}, bf16[128,512]{1,0:T(8,128)(2,1)S(1)}) custom-call(s32[2,8]{1,0:T(2,128)S(1)} %bitcast.14, bf16[1024,512]{1,0:T(8,128)(2,1)} %bitcast.7, bf16[512,512]{1,0:T(8,128)(2,1)} %weight.7, bf16[8,2,128,128]{3,2,1,0:T(8,128)(2,1)} %edges), custom_call_target="tpu_custom_call" | custom-call | flops 939524096 | bytes 4194304 | tf_op jit(solution)/shard_map/pallas_call | solution.py:56
  4.8 0.0 copy-start
  4.8 0.8 collective-permute-start
  5.6 5.6 %collective-permute-start.1 = (bf16[128,512]{1,0:T(8,128)(2,1)S(1)}, bf16[128,512]{1,0:T(8,128)(2,1)S(1)}, u32[]{:S(2)}, u32[]{:S(2)}) collective-permute-start(bf16[128,512]{1,0:T(8,128)(2,1)S(1)} %get-tuple-element.41), channel_id=1, source_target_pairs={{0,1},{2,3},{4,5},{6,7},{8,9},{10,11},{12,13},{14,15},{16,17},{18,... | collective-permute-start | bytes 393224 | tf_op jit(solution)/shard_map/ppermute | solution.py:229
  11.3 0.0 copy-done.2
  11.3 0.0 copy-done.7
  11.3 0.0 copy-done.9
  11.3 0.8 shard_map.122
  12.1 0.0 collective-permute-done.across
  12.1 0.1 collective-permute-done.1.mate
  12.2 0.0 copy-done.6
  12.2 0.0 copy-start.1
  12.2 0.3 shard_map.123
  12.6 0.7 collective-permute-start.2
  13.2 0.0 copy-start.3
  13.2 0.0 copy-start.5
  13.3 5.8 %collective-permute-start.3 = (bf16[128,512]{1,0:T(8,128)(2,1)S(1)}, bf16[128,512]{1,0:T(8,128)(2,1)S(1)}, u32[]{:S(2)}, u32[]{:S(2)}) collective-permute-start(bf16[128,512]{1,0:T(8,128)(2,1)S(1)} %get-tuple-element.46.own), channel_id=1, source_target_pairs={{0,1},{2,3},{4,5},{6,7},{8,9},{10,11},{12,13},{14,15},{16,17},{18,... | collective-permute-start | bytes 393224 | tf_op jit(solution)/shard_map/ppermute | solution.py:229
  19.0 0.0 copy-done
  19.0 0.0 copy-done.1
  19.1 0.9 %shard_map.124.slope = bf16[1024,512]{1,0:T(8,128)(2,1)S(1)} custom-call(bf16[1024,512]{1,0:T(8,128)(2,1)S(1)} %bitcast.8, bf16[512,512]{1,0:T(8,128)(2,1)S(1)} %copy-done.1), custom_call_target="tpu_custom_call" | custom-call | flops 536870912 | bytes 3145728 | tf_op jit(solution)/shard_map/pallas_call | solution.py:56
  20.0 0.0 collective-permute-done.2.across
  20.0 0.0 collective-permute-done.3.mate
  20.0 0.0 copy-done.3
  20.0 0.0 copy-done.5
  20.0 1.1 %shard_map.125 = (bf16[128,512]{1,0:T(8,128)(2,1)}, bf16[128,512]{1,0:T(8,128)(2,1)S(1)}, bf16[128,512]{1,0:T(8,128)(2,1)S(1)}, bf16[128,512]{1,0:T(8,128)(2,1)S(1)}) custom-call(bf16[128,512]{1,0:T(8,128)(2,1)S(1)} %collective-permute-done.2.across, bf16[128,512]{1,0:T(8,128)(2,1)S(1)} %get-tuple-element.46.own, ...), custom_call_target="tpu_custom_call" | custom-call | flops 134217728 | bytes 1048576 | tf_op jit(solution)/shard_map/pallas_call | solution.py:56
  21.1 0.7 collective-permute-start.4
  21.8 5.6 %collective-permute-start.5 = (bf16[128,512]{1,0:T(8,128)(2,1)S(1)}, bf16[128,512]{1,0:T(8,128)(2,1)S(1)}, u32[]{:S(2)}, u32[]{:S(2)}) collective-permute-start(bf16[128,512]{1,0:T(8,128)(2,1)S(1)} %get-tuple-element.55), channel_id=1, source_target_pairs={{0,1},{2,3},{4,5},{6,7},{8,9},{10,11},{12,13},{14,15},{16,17},{18,... | collective-permute-start | bytes 393224 | tf_op jit(solution)/shard_map/ppermute | solution.py:229
  27.4 0.7 shard_map.126.sorted_x
  28.2 0.0 collective-permute-done.4.across
  28.2 0.2 collective-permute-done.5.mate
  28.4 0.0 copy-start.4
  28.4 0.2 shard_map.127
  28.6 0.7 collective-permute-start.6
  29.3 6.9 %collective-permute-start.7 = (bf16[128,512]{1,0:T(8,128)(2,1)S(1)}, bf16[128,512]{1,0:T(8,128)(2,1)S(1)}, u32[]{:S(2)}, u32[]{:S(2)}) collective-permute-start(bf16[128,512]{1,0:T(8,128)(2,1)S(1)} %get-tuple-element.59.own), channel_id=1, source_target_pairs={{0,1},{2,3},{4,5},{6,7},{8,9},{10,11},{12,13},{14,15},{16,17},{18,... | collective-permute-start | bytes 393224 | tf_op jit(solution)/shard_map/ppermute | solution.py:229
  36.2 0.0 copy-done.4
  36.2 0.9 shard_map.128
  37.1 0.0 collective-permute-done.6.across
  37.1 0.1 collective-permute-done.7.mate
  37.2 1.0 %shard_map.129 = (bf16[1024,512]{1,0:T(8,128)(2,1)S(1)}, bf16[256,512]{1,0:T(8,128)(2,1)S(1)}) custom-call(bf16[128,512]{1,0:T(8,128)(2,1)S(1)} %collective-permute-done.6.across, bf16[128,512]{1,0:T(8,128)(2,1)S(1)} %get-tuple-element.59.own, bf16[128,512]{1,0:T(8,128)(2,1)S(1)} %collective-permute-done.7.mate, ...), custom_call_target="tpu_custom_call" | custom-call | flops 671088640 | bytes 4194304 | tf_op jit(solution)/shard_map/pallas_call | solution.py:56
  38.2 2.3 %collective-permute-start.8 = (bf16[256,512]{1,0:T(8,128)(2,1)S(1)}, bf16[256,512]{1,0:T(8,128)(2,1)S(1)}, u32[]{:S(2)}, u32[]{:S(2)}) collective-permute-start(bf16[256,512]{1,0:T(8,128)(2,1)S(1)} %get-tuple-element.68), channel_id=1, source_target_pairs={{0,1},{2,3},{4,5},{6,7},{8,9},{10,11},{12,13},{14,15},{16,17},{18,... | collective-permute-start | bytes 786440 | tf_op jit(solution)/shard_map/ppermute | solution.py:301
  40.4 1.5 %shard_map.130 = (f32[256,512]{1,0:T(8,128)S(1)}, bf16[1024,512]{1,0:T(8,128)(2,1)}) custom-call(bf16[512,1024]{1,0:T(8,128)(2,1)S(1)} %shard_map.126.sorted_x, bf16[1024,512]{1,0:T(8,128)(2,1)S(1)} %get-tuple-element.64.delta, bf16[512,512]{1,0:T(8,128)(2,1)S(1)} %get-tuple-element.65.weight_turned), custom_call_target="tpu_custom_call" | custom-call | flops 805306368 | bytes 4194304 | tf_op jit(solution)/shard_map/pallas_call | solution.py:56
  41.9 0.0 collective-permute-done.8
  41.9 0.1 add_convert_fusion
  42.0 0.1 reshape.9
  42.1 36.7 %all_to_all.10 = bf16[64,4,512]{2,1,0:T(4,128)(2,1)S(1)} all-to-all(bf16[64,4,512]{2,1,0:T(4,128)(2,1)S(1)} %reshape.9), channel_id=1, replica_groups=mesh['ens'=4,'y'=8,'z'=8,'core'=2] {'y','z'}, dimensions={0} | all-to-all | bytes 524288 | tf_op jit(solution)/shard_map/all_to_all | solution.py:311
  78.8 0.1 convert_reduce_fusion
  78.9 8.6 %all_to_all.11 = f32[4,4,512]{2,1,0:T(4,128)S(1)} all-to-all(f32[4,4,512]{2,1,0:T(4,128)S(1)} %broadcast_in_dim.11), channel_id=1, replica_groups=mesh['ens'=4,'y'=8,'z'=8,'core'=2] {'ens'}, dimensions={0} | all-to-all | bytes 65536 | tf_op jit(solution)/shard_map/all_to_all | solution.py:315
  87.6 0.6 reduce_sum.19
  (2 shorter events, 0.0 us)
Async XLA Ops:
  0.6 0.7 copy-start.8
  1.3 10.0 %copy-start.2 = (bf16[512,512]{1,0:T(8,128)(2,1)S(1)}, bf16[512,512]{1,0:T(8,128)(2,1)}, u32[]{:S(2)}) copy-start(bf16[512,512]{1,0:T(8,128)(2,1)} %weight.4) | copy-start | bytes 1572868
  1.3 10.0 %copy-start.7 = (bf16[1,2,128,128]{3,2,1,0:T(8,128)(2,1)S(1)}, bf16[1,2,128,128]{3,2,1,0:T(8,128)(2,1)}, u32[]{:S(2)}) copy-start(bf16[1,2,128,128]{3,2,1,0:T(8,128)(2,1)} %param.15) | copy-start | bytes 196612
  1.3 10.0 %copy-start.9 = (s32[1,2]{1,0:T(1,128)S(1)}, s32[1,2]{1,0:T(1,128)}, u32[]{:S(2)}) copy-start(s32[1,2]{1,0:T(1,128)} %sources) | copy-start | bytes 28
  1.3 10.9 %copy-start.6 = (bf16[1,128,512]{2,1,0:T(8,128)(2,1)S(1)}, bf16[1,128,512]{2,1,0:T(8,128)(2,1)}, u32[]{:S(2)}) copy-start(bf16[1,128,512]{2,1,0:T(8,128)(2,1)} %param.11) | copy-start | bytes 393220
  4.8 14.2 %copy-start = (bf16[1,1024,512]{2,1,0:T(8,128)(2,1)S(1)}, bf16[1,1024,512]{2,1,0:T(8,128)(2,1)}, u32[]{:S(2)}) copy-start(bf16[1,1024,512]{2,1,0:T(8,128)(2,1)} %param.10) | copy-start | bytes 3145732
  4.8 7.3 %collective-permute-start = (bf16[128,512]{1,0:T(8,128)(2,1)S(1)}, bf16[128,512]{1,0:T(8,128)(2,1)S(1)}, u32[]{:S(2)}, u32[]{:S(2)}) collective-permute-start(bf16[128,512]{1,0:T(8,128)(2,1)S(1)} %get-tuple-element.36), channel_id=1, source_target_pairs={{1,2},{3,4},{5,6},{7,8},{9,10},{11,12},{13,14},{15,16},{17,18},{19... | collective-permute-start | bytes 393224 | tf_op jit(solution)/shard_map/ppermute | solution.py:230
  5.6 6.6 %collective-permute-start.1 = (bf16[128,512]{1,0:T(8,128)(2,1)S(1)}, bf16[128,512]{1,0:T(8,128)(2,1)S(1)}, u32[]{:S(2)}, u32[]{:S(2)}) collective-permute-start(bf16[128,512]{1,0:T(8,128)(2,1)S(1)} %get-tuple-element.41), channel_id=1, source_target_pairs={{0,1},{2,3},{4,5},{6,7},{8,9},{10,11},{12,13},{14,15},{16,17},{18,... | collective-permute-start | bytes 393224 | tf_op jit(solution)/shard_map/ppermute | solution.py:229
  12.2 6.8 %copy-start.1 = (bf16[512,512]{1,0:T(8,128)(2,1)S(1)}, bf16[512,512]{1,0:T(8,128)(2,1)}, u32[]{:S(2)}) copy-start(bf16[512,512]{1,0:T(8,128)(2,1)} %weight.7) | copy-start | bytes 1572868
  12.6 7.4 %collective-permute-start.2 = (bf16[128,512]{1,0:T(8,128)(2,1)S(1)}, bf16[128,512]{1,0:T(8,128)(2,1)S(1)}, u32[]{:S(2)}, u32[]{:S(2)}) collective-permute-start(bf16[128,512]{1,0:T(8,128)(2,1)S(1)} %get-tuple-element.42), channel_id=1, source_target_pairs={{1,2},{3,4},{5,6},{7,8},{9,10},{11,12},{13,14},{15,16},{17,18},{19... | collective-permute-start | bytes 393224 | tf_op jit(solution)/shard_map/ppermute | solution.py:230
  13.2 6.8 %copy-start.3 = (bf16[1,128,512]{2,1,0:T(8,128)(2,1)S(1)}, bf16[1,128,512]{2,1,0:T(8,128)(2,1)}, u32[]{:S(2)}) copy-start(bf16[1,128,512]{2,1,0:T(8,128)(2,1)} %param.12) | copy-start | bytes 393220
  13.2 6.8 %copy-start.5 = (bf16[512,512]{1,0:T(8,128)(2,1)S(1)}, bf16[512,512]{1,0:T(8,128)(2,1)}, u32[]{:S(2)}) copy-start(bf16[512,512]{1,0:T(8,128)(2,1)} %weight.6) | copy-start | bytes 1572868
  13.3 6.7 %collective-permute-start.3 = (bf16[128,512]{1,0:T(8,128)(2,1)S(1)}, bf16[128,512]{1,0:T(8,128)(2,1)S(1)}, u32[]{:S(2)}, u32[]{:S(2)}) collective-permute-start(bf16[128,512]{1,0:T(8,128)(2,1)S(1)} %get-tuple-element.46.own), channel_id=1, source_target_pairs={{0,1},{2,3},{4,5},{6,7},{8,9},{10,11},{12,13},{14,15},{16,17},{18,... | collective-permute-start | bytes 393224 | tf_op jit(solution)/shard_map/ppermute | solution.py:229
  21.1 7.1 %collective-permute-start.4 = (bf16[128,512]{1,0:T(8,128)(2,1)S(1)}, bf16[128,512]{1,0:T(8,128)(2,1)S(1)}, u32[]{:S(2)}, u32[]{:S(2)}) collective-permute-start(bf16[128,512]{1,0:T(8,128)(2,1)S(1)} %get-tuple-element.53), channel_id=1, source_target_pairs={{1,2},{3,4},{5,6},{7,8},{9,10},{11,12},{13,14},{15,16},{17,18},{19... | collective-permute-start | bytes 393224 | tf_op jit(solution)/shard_map/ppermute | solution.py:230
  21.8 6.6 %collective-permute-start.5 = (bf16[128,512]{1,0:T(8,128)(2,1)S(1)}, bf16[128,512]{1,0:T(8,128)(2,1)S(1)}, u32[]{:S(2)}, u32[]{:S(2)}) collective-permute-start(bf16[128,512]{1,0:T(8,128)(2,1)S(1)} %get-tuple-element.55), channel_id=1, source_target_pairs={{0,1},{2,3},{4,5},{6,7},{8,9},{10,11},{12,13},{14,15},{16,17},{18,... | collective-permute-start | bytes 393224 | tf_op jit(solution)/shard_map/ppermute | solution.py:229
  28.4 7.8 %copy-start.4 = (bf16[8,2,128,128]{3,2,1,0:T(8,128)(2,1)S(1)}, bf16[8,2,128,128]{3,2,1,0:T(8,128)(2,1)}, u32[]{:S(2)}) copy-start(bf16[8,2,128,128]{3,2,1,0:T(8,128)(2,1)} %edges) | copy-start | bytes 1572868
  28.6 8.4 %collective-permute-start.6 = (bf16[128,512]{1,0:T(8,128)(2,1)S(1)}, bf16[128,512]{1,0:T(8,128)(2,1)S(1)}, u32[]{:S(2)}, u32[]{:S(2)}) collective-permute-start(bf16[128,512]{1,0:T(8,128)(2,1)S(1)} %get-tuple-element.58), channel_id=1, source_target_pairs={{1,2},{3,4},{5,6},{7,8},{9,10},{11,12},{13,14},{15,16},{17,18},{19... | collective-permute-start | bytes 393224 | tf_op jit(solution)/shard_map/ppermute | solution.py:230
  29.3 7.8 %collective-permute-start.7 = (bf16[128,512]{1,0:T(8,128)(2,1)S(1)}, bf16[128,512]{1,0:T(8,128)(2,1)S(1)}, u32[]{:S(2)}, u32[]{:S(2)}) collective-permute-start(bf16[128,512]{1,0:T(8,128)(2,1)S(1)} %get-tuple-element.59.own), channel_id=1, source_target_pairs={{0,1},{2,3},{4,5},{6,7},{8,9},{10,11},{12,13},{14,15},{16,17},{18,... | collective-permute-start | bytes 393224 | tf_op jit(solution)/shard_map/ppermute | solution.py:229
  38.2 3.8 %collective-permute-start.8 = (bf16[256,512]{1,0:T(8,128)(2,1)S(1)}, bf16[256,512]{1,0:T(8,128)(2,1)S(1)}, u32[]{:S(2)}, u32[]{:S(2)}) collective-permute-start(bf16[256,512]{1,0:T(8,128)(2,1)S(1)} %get-tuple-element.68), channel_id=1, source_target_pairs={{0,1},{2,3},{4,5},{6,7},{8,9},{10,11},{12,13},{14,15},{16,17},{18,... | collective-permute-start | bytes 786440 | tf_op jit(solution)/shard_map/ppermute | solution.py:301
